TPU v7x, 256 devices: a whole 4x4x8 slice. The times are simulated.
256 devices in a mesh: tm: 8 (over y, x_hi), inner: 32 (over x_lo, z, core).
Axes of the slice: x: 4 (x_hi: 2, x_lo: 2; x = x_hi * 2 + x_lo), y: 4, z: 8, core: 2. Of those that a mesh axis runs over, the one named last changes fastest.
Arguments:
- frames: bfloat16 [256, 256, 768], P(('tm', 'inner')), may hold values from -6 to 6
- norm_gain: float32 [768], replicated, may hold values from 0.25 to 1.75
- w_qkv: bfloat16 [768, 2304], replicated, may hold values from -16 to 16
- w_out: bfloat16 [768, 768], replicated, may hold values from -0.21875 to 0.21875
- cotangent: bfloat16 [256, 256, 768], P(('tm', 'inner')), may hold values from -24 to 24
Outputs:
- block_out: bfloat16 [256, 256, 768], P(('tm', 'inner'))
- frames_grad: bfloat16 [256, 256, 768], P(('tm', 'inner'))
- qkv_weight_grad: float32 [768, 2304], P('inner', 'tm')
- out_weight_grad: float32 [768, 768], P('inner', 'tm')
- gain_grad: float32 [768], P('inner')
All inputs are finite; a program needn't handle non-finite values.
Results may differ from a plain program's by a relative error of at most 0.012.
The roundings to bfloat16 on the way count: a program that leaves them out, or rounds other values in their place, can miss the bound.
Values may be sent and summed in bfloat16 or wider, within the bound.
A program may use at most 128 MiB of HBM per device.

v0:
```python
import math

import jax
import jax.numpy as jnp
from jax import lax
from jax.sharding import PartitionSpec as P

HEADS = 12
HEAD_DIM = 64
WINDOW = 4
CLIP_MAX = 256


EPSILON = 1e-06


def padded(cells, sides, width):
    for axis, dim in sides:
        count = lax.axis_size(axis)
        ends = count - 1
        head = lax.slice_in_dim(cells, 0, width, axis=dim)
        tail = lax.slice_in_dim(cells, cells.shape[dim] - width, cells.shape[dim], axis=dim)
        cells = jnp.concatenate(
            [
                lax.ppermute(tail, axis, [(i, (i + 1) % count) for i in range(ends)]),
                cells,
                lax.ppermute(head, axis, [((i + 1) % count, i) for i in range(ends)]),
            ],
            axis=dim,
        )
    return cells


def normalize(row_data, norm_gain):
    wide_vals = row_data.astype(jnp.float32)
    center = wide_vals - jnp.mean(wide_vals, axis=-1, keepdims=True)
    spread = lax.rsqrt(jnp.mean(center * center, axis=-1, keepdims=True) + EPSILON)
    unit_rows = center * spread
    return ((unit_rows * norm_gain).astype(jnp.bfloat16), unit_rows, spread)


def norm_back(normed_grad, unit_rows, spread, norm_gain):
    scaled = normed_grad * norm_gain
    mean_one = jnp.mean(scaled, axis=-1, keepdims=True)
    second = jnp.mean(scaled * unit_rows, axis=-1, keepdims=True)
    return spread * (scaled - mean_one - unit_rows * second)


def project(row_data, weight):
    flat_rows = row_data.reshape(-1, row_data.shape[-1])
    result = jnp.dot(flat_rows, weight, preferred_element_type=jnp.float32)
    return result.reshape(row_data.shape[:-1] + (weight.shape[1],))


def project_back(row_data, weight):
    flat_rows = row_data.reshape(-1, row_data.shape[-1])
    result = lax.dot_general(
        flat_rows, weight, (((1,), (1,)), ((), ())), preferred_element_type=jnp.float32
    )
    return result.reshape(row_data.shape[:-1] + (weight.shape[0],))


def contract(left_rows, right_rows):
    left_flat = left_rows.reshape(-1, left_rows.shape[-1])
    right_flat = right_rows.reshape(-1, right_rows.shape[-1])
    return lax.dot_general(
        left_flat, right_flat, (((0,), (0,)), ((), ())), preferred_element_type=jnp.float32
    )


def heads_of(row_data):
    return row_data.reshape(row_data.shape[:-1] + (HEADS, HEAD_DIM))


def attend(query_rows, key_pad, value_pad, first_frame, all_frames, clip_len):
    held_frames = query_rows.shape[0]
    span_len = 2 * WINDOW + 1
    score_scale = HEAD_DIM ** (-0.5)
    query_h = heads_of(query_rows)
    score_list = []
    for offset in range(span_len):
        key_h = heads_of(key_pad[offset : offset + held_frames])
        score_list.append(
            jnp.einsum("ftnd,ftnd->ftn", query_h, key_h, preferred_element_type=jnp.float32)
        )
    scores = jnp.stack(score_list) * score_scale
    query_at = first_frame + jnp.arange(held_frames)[None, :]
    frame_at = query_at + jnp.arange(span_len)[:, None] - WINDOW
    inside = (
        (frame_at >= 0) & (frame_at < all_frames) & (frame_at // clip_len == query_at // clip_len)
    )
    inside = inside[:, :, None, None]
    scores = jnp.where(inside, scores, -1e30)
    row_top = jnp.max(scores, axis=0, keepdims=True)
    exp_scores = jnp.exp(scores - row_top)
    soft_probs = exp_scores / jnp.sum(exp_scores, axis=0, keepdims=True)
    weights_b = soft_probs.astype(jnp.bfloat16)
    mixed_rows = jnp.zeros(query_h.shape, jnp.float32)
    for offset in range(span_len):
        value_h = heads_of(value_pad[offset : offset + held_frames]).astype(jnp.float32)
        mixed_rows = mixed_rows + weights_b[offset][..., None].astype(jnp.float32) * value_h
    mixed_rows = mixed_rows.reshape(query_rows.shape).astype(jnp.bfloat16)
    return (mixed_rows, soft_probs, weights_b)


def attend_back(query_rows, key_pad, value_pad, soft_probs, weights_b, grad_mix):
    held_frames = query_rows.shape[0]
    span_len = 2 * WINDOW + 1
    score_scale = HEAD_DIM ** (-0.5)
    query_h = heads_of(query_rows).astype(jnp.float32)
    grad_h = heads_of(grad_mix)
    dot_list = []
    for offset in range(span_len):
        value_h = heads_of(value_pad[offset : offset + held_frames])
        dot_list.append(
            jnp.einsum("ftnd,ftnd->ftn", grad_h, value_h, preferred_element_type=jnp.float32)
        )
    grad_dots = jnp.stack(dot_list)
    centre = jnp.sum(soft_probs * grad_dots, axis=0, keepdims=True)
    score_grad = (soft_probs * (grad_dots - centre) * score_scale).astype(jnp.bfloat16)
    grad_wide = grad_h.astype(jnp.float32)
    pad_shape = (key_pad.shape[0],) + query_h.shape[1:]
    query_grad = jnp.zeros(query_h.shape, jnp.float32)
    key_grad = jnp.zeros(pad_shape, jnp.float32)
    value_grad = jnp.zeros(pad_shape, jnp.float32)
    for offset in range(span_len):
        key_h = heads_of(key_pad[offset : offset + held_frames]).astype(jnp.float32)
        score_w = score_grad[offset][..., None].astype(jnp.float32)
        query_grad = query_grad + score_w * key_h
        key_grad = key_grad.at[offset : offset + held_frames].add(score_w * query_h)
        value_grad = value_grad.at[offset : offset + held_frames].add(
            weights_b[offset][..., None].astype(jnp.float32) * grad_wide
        )
    flat_shape = (key_pad.shape[0],) + query_rows.shape[1:]
    pad_grad = jnp.concatenate([key_grad.reshape(flat_shape), value_grad.reshape(flat_shape)], -1)
    return (query_grad.reshape(query_rows.shape), pad_grad)


def settle_rims(pad_grad, held_frames):
    edge_rows = jnp.concatenate([pad_grad[:WINDOW], pad_grad[WINDOW + held_frames :]], 0)
    returned = padded(edge_rows.astype(jnp.bfloat16), (("tm", 0),), WINDOW).astype(edge_rows.dtype)
    middle = pad_grad[WINDOW : WINDOW + held_frames]
    middle = middle.at[:WINDOW].add(returned[:WINDOW])
    middle = middle.at[held_frames - WINDOW :].add(returned[3 * WINDOW :])
    return middle


def shards(frames, norm_gain, w_qkv, w_out, cotangent):
    feat_width = frames.shape[-1]
    held_frames = frames.shape[0] * lax.axis_size("inner")
    all_frames = held_frames * lax.axis_size("tm")
    clip_len = min(CLIP_MAX, all_frames)
    first_frame = lax.axis_index("tm") * held_frames
    tokens_all = all_frames * frames.shape[1]
    normed, unit_rows, spread = normalize(frames, norm_gain)
    qkv_rows = project(normed, w_qkv).astype(jnp.bfloat16)
    qkv_tube = lax.all_to_all(qkv_rows, "inner", split_axis=1, concat_axis=0, tiled=True)
    kv_pad = padded(qkv_tube[..., feat_width:], (("tm", 0),), WINDOW)
    query_rows = qkv_tube[..., :feat_width]
    mixed_tube, soft_probs, weights_b = attend(
        query_rows,
        kv_pad[..., :feat_width],
        kv_pad[..., feat_width:],
        first_frame,
        all_frames,
        clip_len,
    )
    mixed_rows = lax.all_to_all(mixed_tube, "inner", split_axis=0, concat_axis=1, tiled=True)
    block_out = (frames.astype(jnp.float32) + project(mixed_rows, w_out)).astype(jnp.bfloat16)
    out_grad = contract(mixed_rows, cotangent)
    grad_mix = project_back(cotangent, w_out).astype(jnp.bfloat16)
    grad_mix_tube = lax.all_to_all(grad_mix, "inner", split_axis=1, concat_axis=0, tiled=True)
    query_grad, pad_grad = attend_back(
        query_rows,
        kv_pad[..., :feat_width],
        kv_pad[..., feat_width:],
        soft_probs,
        weights_b,
        grad_mix_tube,
    )
    kv_grad = settle_rims(pad_grad, held_frames)
    qkv_grad_tube = jnp.concatenate([query_grad, kv_grad], -1).astype(jnp.bfloat16)
    qkv_rows_grad = lax.all_to_all(qkv_grad_tube, "inner", split_axis=0, concat_axis=1, tiled=True)
    qkv_grad = contract(normed, qkv_rows_grad)
    normed_grad = project_back(qkv_rows_grad, w_qkv)
    gain_part = jnp.sum(normed_grad * unit_rows, axis=(0, 1))
    frames_grad = (
        cotangent.astype(jnp.float32) + norm_back(normed_grad, unit_rows, spread, norm_gain)
    ).astype(jnp.bfloat16)
    row_sums = (
        lax.psum_scatter(qkv_grad, "inner", scatter_dimension=0, tiled=True),
        lax.psum_scatter(out_grad, "inner", scatter_dimension=0, tiled=True),
        lax.psum_scatter(gain_part, "inner", scatter_dimension=0, tiled=True),
    )
    qkv_total, out_total = (
        lax.psum_scatter(row_sums[0], "tm", scatter_dimension=1, tiled=True),
        lax.psum_scatter(row_sums[1], "tm", scatter_dimension=1, tiled=True),
    )
    gain_share = lax.psum(row_sums[2], "tm")
    inv_root = 1.0 / math.sqrt(tokens_all)
    return (
        block_out,
        frames_grad,
        qkv_total * inv_root,
        out_total * inv_root,
        gain_share * inv_root,
    )


def solution(mesh):
    in_specs = (P(("tm", "inner"), None, None), P(), P(), P(), P(("tm", "inner"), None, None))
    out_specs = (
        P(("tm", "inner"), None, None),
        P(("tm", "inner"), None, None),
        P("inner", "tm"),
        P("inner", "tm"),
        P("inner"),
    )
    return jax.shard_map(shards, mesh=mesh, in_specs=in_specs, out_specs=out_specs, check_vma=False)
```

profile of v0, /device:TPU:32, one launch (start us, length us, event | category | flops | bytes accessed | tf_op | source)
XLA Modules:
  0.0 812.6 jit_solution(8310351669111820033)
XLA Ops:
  11.2 4.7 reduce.84
  17.8 10.1 %all-to-all-start.2 = ((bf16[32,2,3072]{2,1,0:T(2,128)(2,1)}), bf16[32,2,3072]{2,1,0:T(2,128)(2,1)}, u32[]{:S(2)}, u32[]{:S(2)}) async-start(bf16[32,2,3072]{2,1,0:T(2,128)(2,1)} %reshape.1221), calls=%async_computation.2 | async-start | bytes 786432 | tf_op jit(solution)/shard_map/all_to_all | solution.py:172
  32.5 3.2 copy.167
  35.7 9.9 %reduce.83 = bf16[256,2304]{1,0:T(8,128)(2,1)} reduce(bf16[256,1,2304]{2,1,0:T(2,128)(2,1)} %bitcast.189, bf16[]{:T(256)} %broadcast.461), dimensions={1}, to_apply=%bitcast.182.reduce_sub_computation | reduce | bytes 2359298
  45.6 3.9 reshape.1219
  49.4 9.0 %all-to-all-start = ((bf16[32,2,9216]{2,1,0:T(2,128)(2,1)}), bf16[32,2,9216]{2,1,0:T(2,128)(2,1)}, u32[]{:S(2)}, u32[]{:S(2)}) async-start(bf16[32,2,9216]{2,1,0:T(2,128)(2,1)} %reshape.1219), calls=%async_computation | async-start | bytes 2359296 | tf_op jit(solution)/shard_map/all_to_all | solution.py:157
  58.5 3.4 reshape.1222
  61.9 4.2 bitcast_reduce_fusion
  68.6 21.6 %all-to-all-done = bf16[32,2,9216]{2,1,0:T(2,128)(2,1)} async-done(((bf16[32,2,9216]{2,1,0:T(2,128)(2,1)}), bf16[32,2,9216]{2,1,0:T(2,128)(2,1)}, u32[]{:S(2)}, u32[]{:S(2)}) %all-to-all-start) | async-done | bytes 1179680 | tf_op jit(solution)/shard_map/all_to_all | solution.py:157
  90.1 5.8 reshape.1220
  98.5 5.3 collective-permute-start
  114.4 3.7 fusion.80
  137.7 8.8 %fusion.9 = (f32[32,8,12]{2,1,0:T(8,128)}, f32[32,8,12]{2,1,0:T(8,128)}, f32[32,8,12]{2,1,0:T(8,128)}, f32[32,8,12]{2,1,0:T(8,128)}, f32[32,8,12]{2,1,0:T(8,128)...) fusion(bf16[32,8,12,64]{3,2,1,0:T(8,128)(2,1)} %reshape.1114, ...), kind=kLoop, calls=%fused_computation.60 | loop fusion | flops 5477376 | bytes 4042752
  190.8 3.2 convert_multiply_fusion.8
  198.7 3.6 scatter-add.81
  202.3 3.0 fusion.36
  209.9 3.4 fusion.38
  215.3 2.8 mul.400
  218.0 3.4 fusion.40
  226.1 3.3 fusion.42
  234.1 3.4 fusion.44
  239.4 2.7 mul.409
  242.1 3.4 fusion.46
  250.2 3.5 fusion.48
  255.6 2.7 mul.415
  259.9 2.9 mul.417
  265.4 6.2 add_convert_fusion.1
  291.2 10.7 %fusion.34 = (f32[32,8,12]{2,1,0:T(8,128)}, f32[32,8,12]{2,1,0:T(8,128)}, f32[32,8,12]{2,1,0:T(8,128)}, f32[32,8,12]{2,1,0:T(8,128)}, f32[32,8,12]{2,1,0:T(8,128...) fusion(bf16[32,8,12,64]{3,2,1,0:T(8,128)(2,1)} %reshape.1127, ...), kind=kLoop, calls=%fused_computation.85 | loop fusion | flops 5870592 | bytes 15990784
  349.0 4.4 all-to-all-start.1
  353.5 3.4 fusion.11
  356.9 3.1 fusion.13
  359.9 3.1 fusion.15
  363.0 3.0 fusion.17
  366.0 3.0 fusion.19
  369.1 3.0 fusion.21
  372.1 2.9 fusion.23
  376.6 3.2 fusion.25
  379.8 2.9 reshape.1137
  382.7 2.9 reshape.1138
  389.6 3.0 fusion.87
  394.3 3.0 mul.423
  397.3 2.9 mul.424
  400.2 3.0 mul.426
  403.2 2.8 mul.427
  406.0 2.9 mul.429
  411.5 2.8 mul.432
  414.3 2.7 mul.433
  417.1 2.8 mul.435
  422.6 2.8 mul.438
  428.1 2.8 mul.441
  433.6 2.9 mul.444
  436.5 2.7 mul.445
  439.2 2.8 mul.447
  442.1 2.7 mul.448
  444.8 6.1 collective-permute-start.2
  452.3 4.7 add_convert_fusion
  459.5 41.3 %all_to_all.19 = bf16[32,8,2304]{2,1,0:T(8,128)(2,1)S(1)} all-to-all(bf16[32,8,2304]{2,1,0:T(8,128)(2,1)S(1)} %pad_maximum_fusion), channel_id=1, replica_groups=mesh['tm'=8,'inner'=32] {'inner'}, dimensions={0} | all-to-all | bytes 2359296 | tf_op jit(solution)/shard_map/all_to_all | solution.py:183
  501.8 4.1 fusion.54
  507.9 2.8 fusion.52
  513.3 49.7 %all-reduce.2 = f32[768]{0:T(1024)} all-reduce(f32[768]{0:T(1024)S(1)} %get-tuple-element.245), channel_id=6, replica_groups=mesh['tm'=8,'inner'=32] {'inner'}, use_global_device_ids=true, to_apply=%region_12.13.clone | all-reduce | flops 768 | bytes 6144
  563.8 25.3 %psum.7 = f32[24]{0:T(128)} all-reduce(f32[24]{0:T(128)S(1)} %dynamic-slice.159), channel_id=1, replica_groups=mesh['tm'=8,'inner'=32] {'tm'}, use_global_device_ids=true, to_apply=%region_13.14 | all-reduce | flops 24 | bytes 192 | tf_op jit(solution)/shard_map/psum | solution.py:199
  596.0 47.4 %reduce-scatter.9.cloned.1.call-done = f32[24,2304]{1,0:T(8,128)} async-done(((f32[768,2304]{1,0:T(8,128)}), f32[24,2304]{1,0:T(8,128)}) %reduce-scatter.9.cloned.1.call-update) | async-done | bytes 221200 | tf_op jit(solution)/shard_map/reduce_scatter | solution.py:191
  646.9 75.1 %reduce-scatter.15.cloned.1.call-done = f32[96,24]{1,0:T(8,128)} async-done(((f32[768,24]{1,0:T(8,128)}), f32[96,24]{1,0:T(8,128)}) %reduce-scatter.15.cloned.1.call-update) | async-done | bytes 9232
  723.5 79.4 %reduce-scatter.13.cloned.1.call-done = f32[288,24]{1,0:T(8,128)} async-done(((f32[2304,24]{1,0:T(8,128)}), f32[288,24]{1,0:T(8,128)}) %reduce-scatter.13.cloned.1.call-update) | async-done | bytes 27664
  (220 shorter events, 232.4 us)
Async XLA Ops:
  7.2 23.2 %copy-start = (bf16[768,2304]{1,0:T(8,128)(2,1)S(1)}, bf16[768,2304]{1,0:T(8,128)(2,1)}, u32[]{:S(2)}) copy-start(bf16[768,2304]{1,0:T(8,128)(2,1)} %param.47) | copy-start | bytes 10616836
  9.2 21.1 %copy-start.30 = (f32[768]{0:T(1024)S(1)}, f32[768]{0:T(1024)}, u32[]{:S(2)}) copy-start(f32[768]{0:T(1024)} %param.46) | copy-start | bytes 9220
  17.8 31.6 %all-to-all-start.2 = ((bf16[32,2,3072]{2,1,0:T(2,128)(2,1)}), bf16[32,2,3072]{2,1,0:T(2,128)(2,1)}, u32[]{:S(2)}, u32[]{:S(2)}) async-start(bf16[32,2,3072]{2,1,0:T(2,128)(2,1)} %reshape.1221), calls=%async_computation.2 | async-start | bytes 786432 | tf_op jit(solution)/shard_map/all_to_all | solution.py:172
  49.4 40.7 %all-to-all-start = ((bf16[32,2,9216]{2,1,0:T(2,128)(2,1)}), bf16[32,2,9216]{2,1,0:T(2,128)(2,1)}, u32[]{:S(2)}, u32[]{:S(2)}) async-start(bf16[32,2,9216]{2,1,0:T(2,128)(2,1)} %reshape.1219), calls=%async_computation | async-start | bytes 2359296 | tf_op jit(solution)/shard_map/all_to_all | solution.py:157
  97.7 9.4 %copy-start.3 = (bf16[1,256,2304]{2,1,0:T(8,128)(2,1)}, bf16[1,256,2304]{2,1,0:T(8,128)(2,1)S(1)}, u32[]{:S(2)}) copy-start(bf16[1,256,2304]{2,1,0:T(8,128)(2,1)S(1)} %copy.166) | copy-start | bytes 3538948
  98.5 15.9 %collective-permute-start = (bf16[4,8,1536]{2,1,0:T(8,128)(2,1)}, bf16[4,8,1536]{2,1,0:T(8,128)(2,1)}, u32[]{:S(2)}, u32[]{:S(2)}) collective-permute-start(bf16[4,8,1536]{2,1,0:T(8,128)(2,1)} %get-tuple-element.277), channel_id=1, source_target_pairs={{0,32},{32,64},{64,96},{96,128},{128,160},{160,192},{192,224},{1,3... | collective-permute-start | bytes 294920 | tf_op jit(solution)/shard_map/ppermute | solution.py:25
  103.8 10.6 %collective-permute-start.1 = (bf16[4,8,1536]{2,1,0:T(8,128)(2,1)}, bf16[4,8,1536]{2,1,0:T(8,128)(2,1)}, u32[]{:S(2)}, u32[]{:S(2)}) collective-permute-start(bf16[4,8,1536]{2,1,0:T(8,128)(2,1)} %get-tuple-element.278), channel_id=1, source_target_pairs={{32,0},{64,32},{96,64},{128,96},{160,128},{192,160},{224,192},{33,... | collective-permute-start | bytes 294920 | tf_op jit(solution)/shard_map/ppermute | solution.py:27
  175.1 1.2 copy-start.12
  176.3 2.0 copy-start.29
  190.8 3.2 copy-start.13
  198.7 3.6 copy-start.2
  198.7 3.6 copy-start.26
  209.9 3.4 copy-start.25
  218.0 3.4 copy-start.24
  226.1 3.4 copy-start.23
  234.1 3.4 copy-start.22
  242.1 3.4 copy-start.21
  250.2 3.5 copy-start.20
  318.0 12.7 %copy-start.4 = (f32[9,32,8,12]{1,2,3,0:T(8,128)S(1)}, f32[9,32,8,12]{1,2,3,0:T(8,128)}, u32[]{:S(2)}) copy-start(f32[9,32,8,12]{1,2,3,0:T(8,128)} %bitcast_dynamic-update-slice_fusion.9) | copy-start | bytes 331780
  349.0 40.5 %all-to-all-start.1 = ((bf16[32,8,768]{2,1,0:T(8,128)(2,1)}), bf16[32,8,768]{2,1,0:T(8,128)(2,1)}, u32[]{:S(2)}, u32[]{:S(2)}) async-start(bf16[32,8,768]{2,1,0:T(8,128)(2,1)} %get-tuple-element.265), calls=%async_computation.1 | async-start | bytes 786432 | tf_op jit(solution)/shard_map/all_to_all | solution.py:168
  353.4 238.2 %reduce-scatter.11.cloned.1.call-start = ((), (), s32[]{:S(2)}) async-start(), calls=%async_computation.9 | async-start | bytes 2433024 | tf_op jit(solution)/shard_map/reduce_scatter | solution.py:192
  353.5 3.4 copy-start.1
  353.5 3.4 copy-start.19
  356.9 3.1 copy-start.18
  359.9 3.1 copy-start.17
  363.0 3.0 copy-start.16
  366.0 3.0 copy-start.15
  369.1 3.0 copy-start.14
  385.5 1.5 copy-start.11
  387.2 1.3 copy-start.5
  392.6 250.8 %reduce-scatter.9.cloned.1.call-start = ((), (), s32[]{:S(2)}) async-start(), calls=%async_computation.8 | async-start | bytes 7299072 | tf_op jit(solution)/shard_map/reduce_scatter | solution.py:191
  444.8 12.4 %collective-permute-start.2 = (bf16[4,8,1536]{2,1,0:T(8,128)(2,1)}, bf16[4,8,1536]{2,1,0:T(8,128)(2,1)S(1)}, u32[]{:S(2)}, u32[]{:S(2)}) collective-permute-start(bf16[4,8,1536]{2,1,0:T(8,128)(2,1)} %get-tuple-element.280), channel_id=1, source_target_pairs={{0,32},{32,64},{64,96},{96,128},{128,160},{160,192},{192,224},{1,3... | collective-permute-start | bytes 294920 | tf_op jit(solution)/shard_map/ppermute | solution.py:25
  450.9 6.2 copy-start.6
  450.9 8.4 %collective-permute-start.3 = (bf16[4,8,1536]{2,1,0:T(8,128)(2,1)}, bf16[4,8,1536]{2,1,0:T(8,128)(2,1)S(1)}, u32[]{:S(2)}, u32[]{:S(2)}) collective-permute-start(bf16[4,8,1536]{2,1,0:T(8,128)(2,1)} %get-tuple-element.281), channel_id=1, source_target_pairs={{32,0},{64,32},{96,64},{128,96},{160,128},{192,160},{224,192},{33,... | collective-permute-start | bytes 294920 | tf_op jit(solution)/shard_map/ppermute | solution.py:27
  457.1 2.2 copy-start.27
  457.1 2.2 copy-start.28
  459.4 42.4 %copy-start.7 = (bf16[1,256,768]{2,1,0:T(8,128)(2,1)S(1)}, bf16[1,256,768]{2,1,0:T(8,128)(2,1)}, u32[]{:S(2)}) copy-start(bf16[1,256,768]{2,1,0:T(8,128)(2,1)} %param.45) | copy-start | bytes 1179652
  500.8 1.0 copy-start.9
  506.0 0.7 copy-start.31
  506.0 216.1 %reduce-scatter.15.cloned.1.call-start = ((), (), s32[]{:S(2)}) async-start(), calls=%async_computation.11 | async-start | bytes 442368
  507.9 2.8 copy-start.8
  507.9 2.8 copy-start.10
  593.5 209.4 %reduce-scatter.13.cloned.1.call-start = ((), (), s32[]{:S(2)}) async-start(), calls=%async_computation.10 | async-start | bytes 1327104
Sparse Core Ops, SparseCore 0:
  392.8 122.8 reduce-scatter.10
  518.3 125.0 reduce-scatter.8
  647.2 74.7 reduce-scatter.14
  725.8 76.9 reduce-scatter.12
where the time goes:
time: 822 us; the launch traced here: 813 us
  local copies, waits for them, and re-layouts  280 us (34%)
  waiting for transfers between devices  226 us (27%)
  other arithmetic  121 us (15%)
  blocking collectives  116 us (14%)
  starting transfers between devices  37.9 us (5%)
  matrix products  16.8 us (2%)
  between operations  15.1 us (2%)
    unnamed x6, waiting for transfers between devices  155 us
    unnamed x93, local copies, waits for them, and re-layouts  52.3 us
    mul x18, local copies, waits for them, and re-layouts, attend_back(): query_grad = query_grad + score_w * key_h  50.4 us
    unnamed x1, blocking collectives  49.7 us
    reshape x20, local copies, waits for them, and re-layouts, heads_of(): return row_data.reshape(row_data.shape[:-1] + (HEADS, HEAD_DIM))  48.9 us
    reduce_scatter x1, waiting for transfers between devices, shards(): lax.psum_scatter(qkv_grad, 'inner', scatter_dimension=0, tiled=True)  47.4 us
    mul x18, local copies, waits for them, and re-layouts, attend(): weights_b[offset][..., None].astype(jnp.float32) * value_h  42.8 us
    all_to_all x1, blocking collectives, shards(): lax.all_to_all(qkv_grad_tube, 'inner', split_axis=0, concat_axis=1, tiled...  41.3 us
  transfers between devices with their start and end apart: 11, of which 5 were waited for; matrix products, arithmetic and copies ran while one was open for 19% of the time, Pallas kernels for 0%

commit v1 on v0

v1 whole, which is shorter than its diff:
```python
import functools
import math

import jax
import jax.numpy as jnp
from jax import lax
from jax.experimental import pallas as pl
from jax.experimental.pallas import tpu as pltpu
from jax.sharding import PartitionSpec as P

HEAD_DIM = 64
WINDOW = 4
CLIP_MAX = 256
EPSILON = 1e-06
SPAN = 2 * WINDOW + 1
WIDE = 128
CORES = 2
X_LO = 2
X_HI = 2
MESH = pl.DeviceIdType.MESH
F32 = jnp.float32
BF16 = jnp.bfloat16


def dot(a, b, dims=((1,), (0,))):
    return lax.dot_general(a, b, (dims, ((), ())), preferred_element_type=F32)


def split(wide_vals):
    high = wide_vals.astype(BF16)
    low = (wide_vals - high.astype(F32)).astype(BF16)
    return jnp.concatenate([high, low], axis=1)


def attention_kernel(
    sizes,
    x_ref,
    gain_ref,
    wqkv_ref,
    wout_ref,
    cot_ref,
    bo_ref,
    fg_ref,
    nrm_ref,
    mix_ref,
    dqkv_ref,
    gg_ref,
    halo,
    comp,
    rcomp,
    wd,
    unit,
    spread,
    ones,
    pick,
    spill,
    send_sem,
    recv_sem,
    csend_sem,
    crecv_sem,
):
    frames_all, inner, clip = sizes
    tokens, width = x_ref.shape
    chunks = width // WIDE
    rows_tile = 64
    f = lax.axis_index("tm") * inner + lax.axis_index("inner")
    odd = lax.rem(f, 2)

    def at(offset):
        g = lax.rem(f + offset + frames_all, frames_all)
        return (lax.div(g, inner), lax.rem(g, inner))

    others = [j for j in range(-WINDOW, WINDOW + 1) if j != 0]
    barrier = pltpu.get_barrier_semaphore()
    for j in others:
        pl.semaphore_signal(barrier, inc=1, device_id=at(j), device_id_type=MESH)

    wide_vals = x_ref[...].astype(F32)
    center = wide_vals - jnp.mean(wide_vals, axis=-1, keepdims=True)
    spread_one = lax.rsqrt(jnp.mean(center * center, axis=-1, keepdims=True) + EPSILON)
    unit_rows = center * spread_one
    unit[...] = unit_rows
    spread[...] = spread_one
    nrm_ref[...] = (unit_rows * gain_ref[...]).astype(BF16)

    row_at = lax.broadcasted_iota(jnp.int32, (2 * WIDE, WIDE), 0)
    lane_at = lax.broadcasted_iota(jnp.int32, (2 * WIDE, WIDE), 1)
    same = (lax.rem(row_at, WIDE) // HEAD_DIM) == (lane_at // HEAD_DIM)
    ones[...] = jnp.where(same, 1.0, 0.0).astype(BF16)
    row_at = lax.broadcasted_iota(jnp.int32, (16, 2 * WIDE), 0)
    lane_at = lax.broadcasted_iota(jnp.int32, (16, 2 * WIDE), 1)
    pick[...] = jnp.where(lane_at == row_at * HEAD_DIM, 1.0, 0.0).astype(BF16)
    spill[...] = jnp.where(lane_at // HEAD_DIM == row_at, 1.0, 0.0).astype(BF16)

    pl.semaphore_wait(barrier, len(others))

    def copy(c, k):
        if k < 4:
            source = (4, 4, 2, 6)[k]
            target = (2, 6, 0, 8)[k]
            where = at((2, -2, 2, -2)[k])
        else:
            source = (4, 2, 6, 8 - 8 * odd)[k - 4]
            target = source - 1 + 2 * odd
            where = at(1 - 2 * odd)
        return pltpu.make_async_remote_copy(
            src_ref=halo.at[c, source],
            dst_ref=halo.at[c, target],
            send_sem=send_sem.at[c, k],
            recv_sem=recv_sem.at[c, k],
            device_id=where,
            device_id_type=MESH,
        )

    def comp_copy(c, j):
        k = j + WINDOW
        return pltpu.make_async_remote_copy(
            src_ref=comp.at[c, k],
            dst_ref=rcomp.at[c, SPAN - 1 - k],
            send_sem=csend_sem.at[c, k],
            recv_sem=crecv_sem.at[c, k],
            device_id=at(j),
            device_id_type=MESH,
        )

    def columns(c, part):
        return pl.ds(pl.multiple_of(part * width + c * WIDE, WIDE), WIDE)

    def project(c):
        for part in range(3):
            result = dot(nrm_ref[...], wqkv_ref[:, columns(c, part)])
            halo[c, 4, :, part * WIDE : (part + 1) * WIDE] = result.astype(BF16)
        rows = pl.ds(pl.multiple_of(c * WIDE, WIDE), WIDE)
        result = dot(cot_ref[...], wout_ref[rows, :], ((1,), (1,)))
        halo[c, 4, :, 3 * WIDE : 4 * WIDE] = result.astype(BF16)
        for k in (0, 1, 4):
            copy(c, k).start()

    def relay(c):
        copy(c, 0).wait_recv()
        copy(c, 2).start()
        copy(c, 5).start()
        copy(c, 1).wait_recv()
        copy(c, 3).start()
        copy(c, 6).start()

    def relay_last(c):
        copy(c, 2).wait_recv()
        copy(c, 3).wait_recv()
        copy(c, 7).start()

    def attend(c):
        for k in (4, 5, 6, 7):
            copy(c, k).wait_recv()

        @pl.loop(0, tokens // rows_tile)
        def _(i):
            rows = pl.ds(pl.multiple_of(i * rows_tile, rows_tile), rows_tile)
            query = halo[c, 4, rows, 0:WIDE].astype(F32)
            grad = halo[c, 4, rows, 3 * WIDE : 4 * WIDE].astype(F32)
            products = []
            for k in range(SPAN):
                products.append(split(query * halo[c, k, rows, WIDE : 2 * WIDE].astype(F32)))
            scores = dot(jnp.concatenate(products, axis=0), ones[...]) * (HEAD_DIM**-0.5)
            products = []
            for k in range(SPAN):
                products.append(
                    split(grad * halo[c, k, rows, 2 * WIDE : 3 * WIDE].astype(F32))
                )
            dots = dot(jnp.concatenate(products, axis=0), ones[...])
            score = []
            for k in range(SPAN):
                g = f + (k - WINDOW)
                inside = (g >= 0) & (g < frames_all)
                inside = inside & (lax.div(g + clip, clip) == lax.div(f + clip, clip))
                cap = jnp.where(inside, 3e38, -1e30).astype(F32)
                score.append(jnp.minimum(scores[k * rows_tile : (k + 1) * rows_tile], cap))
            top = functools.reduce(jnp.maximum, score)
            raised = [jnp.exp(s - top) for s in score]
            scale = 1.0 / functools.reduce(jnp.add, raised)
            soft = [e * scale for e in raised]
            mixed = jnp.zeros((rows_tile, WIDE), F32)
            centre = jnp.zeros((rows_tile, WIDE), F32)
            for k in range(SPAN):
                weight = soft[k].astype(BF16)
                wd[k, rows, 0:WIDE] = weight
                mixed += weight.astype(F32) * halo[c, k, rows, 2 * WIDE : 3 * WIDE].astype(F32)
                centre += soft[k] * dots[k * rows_tile : (k + 1) * rows_tile]
            mix_ref[rows, columns(c, 0)] = mixed.astype(BF16)
            query_grad = jnp.zeros((rows_tile, WIDE), F32)
            for k in range(SPAN):
                gap = dots[k * rows_tile : (k + 1) * rows_tile] - centre
                slope = (soft[k] * gap * (HEAD_DIM**-0.5)).astype(BF16)
                wd[k, rows, WIDE : 2 * WIDE] = slope
                query_grad += slope.astype(F32) * halo[c, k, rows, WIDE : 2 * WIDE].astype(F32)
            dqkv_ref[rows, columns(c, 0)] = query_grad.astype(BF16)

        for k in range(SPAN):
            small = dot(pick[...], wd[k], ((1,), (1,))).astype(BF16)
            if k == WINDOW:
                rcomp[c, k] = small
            else:
                comp[c, k] = small
                comp_copy(c, k - WINDOW).start()

    def collect(c):
        for j in others:
            comp_copy(c, j).wait_recv()
        half = 128
        for i in range(tokens // half):
            rows = slice(i * half, (i + 1) * half)
            key_grad = jnp.zeros((half, WIDE), F32)
            value_grad = jnp.zeros((half, WIDE), F32)
            for k in range(SPAN):
                wide = dot(rcomp[c, k, :, rows], spill[...], ((0,), (0,)))
                value_grad += wide[:, :WIDE] * halo[c, k, rows, 3 * WIDE : 4 * WIDE].astype(F32)
                key_grad += wide[:, WIDE:] * halo[c, k, rows, 0:WIDE].astype(F32)
            dqkv_ref[rows, columns(c, 1)] = key_grad.astype(BF16)
            dqkv_ref[rows, columns(c, 2)] = value_grad.astype(BF16)

    ahead = min(3, chunks)

    @pl.loop(0, ahead)
    def _(c):
        project(c)

    relay(0)

    @pl.loop(0, chunks + 1)
    def _(c):
        @pl.when(c + ahead < chunks)
        def _():
            project(c + ahead)

        @pl.when(c + 1 < chunks)
        def _():
            relay(c + 1)

        @pl.when(c < chunks)
        def _():
            relay_last(c)
            attend(c)

        @pl.when(c == chunks)
        def _():
            mixed_out = dot(mix_ref[...], wout_ref[...])
            bo_ref[...] = (x_ref[...].astype(F32) + mixed_out).astype(BF16)

        @pl.when(c > 0)
        def _():
            collect(c - 1)

    normed_grad = dot(dqkv_ref[...], wqkv_ref[...], ((1,), (1,)))
    unit_rows = unit[...]
    gain_part = jnp.sum(normed_grad * unit_rows, axis=0, keepdims=True)
    gg_ref[...] = jnp.zeros(gg_ref.shape, F32)
    for i in range(chunks):
        gg_ref[i : i + 1, :] = gain_part[:, i * WIDE : (i + 1) * WIDE]
    scaled = normed_grad * gain_ref[...]
    mean_one = jnp.mean(scaled, axis=-1, keepdims=True)
    second = jnp.mean(scaled * unit_rows, axis=-1, keepdims=True)
    back = spread[...] * (scaled - mean_one - unit_rows * second)
    fg_ref[...] = (cot_ref[...].astype(F32) + back).astype(BF16)

    @pl.loop(0, chunks)
    def _(c):
        for k in range(8):
            copy(c, k).wait_send()
        for j in others:
            comp_copy(c, j).wait_send()


def attention(mesh_sizes, x, gain, w_qkv, w_out, cot):
    tm_size, inner = mesh_sizes
    tokens, width = x.shape
    chunks = width // WIDE
    frames_all = tm_size * inner
    vmem = pl.BlockSpec(memory_space=pltpu.VMEM)
    sizes = (frames_all, inner, min(CLIP_MAX, frames_all))
    return pl.pallas_call(
        functools.partial(attention_kernel, sizes),
        out_shape=(
            jax.ShapeDtypeStruct((tokens, width), BF16),
            jax.ShapeDtypeStruct((tokens, width), BF16),
            jax.ShapeDtypeStruct((tokens, width), BF16),
            jax.ShapeDtypeStruct((tokens, width), BF16),
            jax.ShapeDtypeStruct((tokens, 3 * width), BF16),
            jax.ShapeDtypeStruct((8, WIDE), F32),
        ),
        in_specs=[vmem] * 5,
        out_specs=(vmem,) * 6,
        scratch_shapes=[
            pltpu.VMEM((chunks, SPAN, tokens, 4 * WIDE), BF16),
            pltpu.VMEM((chunks, SPAN, 16, tokens), BF16),
            pltpu.VMEM((chunks, SPAN, 16, tokens), BF16),
            pltpu.VMEM((SPAN, tokens, 2 * WIDE), BF16),
            pltpu.VMEM((tokens, width), F32),
            pltpu.VMEM((tokens, 1), F32),
            pltpu.VMEM((2 * WIDE, WIDE), BF16),
            pltpu.VMEM((16, 2 * WIDE), BF16),
            pltpu.VMEM((16, 2 * WIDE), BF16),
            pltpu.SemaphoreType.DMA((chunks, 8)),
            pltpu.SemaphoreType.DMA((chunks, 8)),
            pltpu.SemaphoreType.DMA((chunks, SPAN)),
            pltpu.SemaphoreType.DMA((chunks, SPAN)),
        ],
        compiler_params=pltpu.CompilerParams(
            collective_id=0, has_side_effects=True, vmem_limit_bytes=56 * 2**20
        ),
        name="windowed_attention",
    )(x, gain, w_qkv, w_out, cot)


def reduce_kernel(
    sizes,
    nrm_ref,
    mix_ref,
    right_ref,
    gain_ref,
    out_ref,
    gout_ref,
    core_send,
    core_recv,
    total,
    first_send,
    first_recv,
    next_total,
    next_send,
    next_recv,
    z_total,
    z_send,
    z_recv,
    final_send,
    final_recv,
    gain_core,
    gain_y,
    gain_x,
    gain_z,
    core_ssem,
    core_rsem,
    first_ssem,
    first_rsem,
    next_ssem,
    next_rsem,
    z_ssem,
    z_rsem,
    final_ssem,
    final_rsem,
    gain_ssem,
    gain_rsem,
):
    ny, nx, nz, left_width, inv_root = sizes
    halves = CORES
    rows = total.shape[1]
    part = rows // 2
    z_half = nz // halves
    z_rows = rows // z_half
    blocks = ny * nx
    tm_at = lax.axis_index("tm")
    inner_at = lax.axis_index("inner")
    core = lax.rem(inner_at, CORES)
    z = lax.rem(lax.div(inner_at, CORES), nz)
    x = lax.rem(tm_at, X_HI) * X_LO + lax.div(inner_at, CORES * nz)
    y = lax.div(tm_at, X_HI)

    def device(yy, xx, zz, cc):
        return (
            yy * X_HI + lax.div(xx, X_LO),
            (lax.rem(xx, X_LO) * nz + zz) * CORES + cc,
        )

    def turned(value, step, count):
        return lax.rem(value + step, count)

    peers = [device(y, x, z, 1 - core)]
    peers += [device(turned(y, d, ny), x, z, core) for d in range(1, ny)]
    peers += [device(y, turned(x, d, nx), z, core) for d in range(1, nx)]
    peers += [device(y, x, turned(z, d, nz), core) for d in range(1, nz)]
    barrier = pltpu.get_barrier_semaphore()
    for peer in peers:
        pl.semaphore_signal(barrier, inc=1, device_id=peer, device_id_type=MESH)
    pl.semaphore_wait(barrier, len(peers))

    def remote(source, target, ssem, rsem, where):
        return pltpu.make_async_remote_copy(
            src_ref=source,
            dst_ref=target,
            send_sem=ssem,
            recv_sem=rsem,
            device_id=where,
            device_id_type=MESH,
        )

    def gain_exchange(buffer, own, count, spot, slot):
        moves = []
        for d in range(1, count):
            moves.append(
                remote(
                    buffer.at[own],
                    buffer.at[own],
                    gain_ssem.at[slot, d],
                    gain_rsem.at[slot, d],
                    spot(turned(own, d, count)),
                )
            )
        return moves

    def gain_sum(buffer, count):
        value = buffer[0]
        for i in range(1, count):
            value = value + buffer[i]
        return value

    def weight_block(b, half):
        yy, xx = lax.div(b, nx), lax.rem(b, nx)
        t = yy * X_HI + lax.div(xx, X_LO)
        lo = lax.rem(xx, X_LO)
        right = right_ref[t]
        first = dot(nrm_ref[lo, half], right)
        second = dot(mix_ref[lo, half], right)
        lane = lax.broadcasted_iota(jnp.int32, first.shape, 1)
        return jnp.where(lane < left_width, first, second)

    def core_copy(b):
        return remote(
            core_send.at[b],
            core_recv.at[b],
            core_ssem.at[b],
            core_rsem.at[b],
            device(y, x, z, 1 - core),
        )

    gain_core[core] = gain_ref[...]
    core_gain = gain_exchange(
        gain_core, core, CORES, lambda cc: device(y, x, z, cc), 0
    )
    for move in core_gain:
        move.start()

    @pl.loop(0, blocks)
    def _(b):
        core_send[b] = weight_block(b, 1 - core).astype(BF16)
        core_copy(b).start()

    def first_copy(side, yy, xx):
        if side == 0:
            own, goal, line = y, yy, xx
            where = device(yy, x, z, core)
        else:
            own, goal, line = x, xx, yy
            where = device(y, xx, z, core)
        return remote(
            first_send.at[side, goal, line],
            first_recv.at[side, own, line],
            first_ssem.at[side, goal, line],
            first_rsem.at[side, own, line],
            where,
        )

    @pl.loop(0, blocks)
    def _(b):
        yy, xx = lax.div(b, nx), lax.rem(b, nx)
        own = weight_block(b, core)
        core_copy(b).wait_recv()
        own = own + core_recv[b].astype(F32)
        total[b] = own
        first_send[0, yy, xx] = own[:part].astype(BF16)
        first_send[1, xx, yy] = own[part:].astype(BF16)

        @pl.when(yy != y)
        def _():
            first_copy(0, yy, xx).start()

        @pl.when(xx != x)
        def _():
            first_copy(1, yy, xx).start()

    for move in core_gain:
        move.wait_recv()
    gain_y[y] = gain_sum(gain_core, CORES)
    y_gain = gain_exchange(gain_y, y, ny, lambda yy: device(yy, x, z, core), 1)
    for move in y_gain:
        move.start()

    def first_wait(side, d, line):
        own, count = (y, ny) if side == 0 else (x, nx)
        sender = turned(own, d, count)
        return sender, remote(
            first_send.at[side, sender, line],
            first_recv.at[side, sender, line],
            first_ssem.at[side, sender, line],
            first_rsem.at[side, sender, line],
            device(y, x, z, 1 - core),
        )

    def next_copy(side, d):
        if side == 0:
            own, goal = x, turned(x, d, nx)
            where = device(y, goal, z, core)
        else:
            own, goal = y, turned(y, d, ny)
            where = device(goal, x, z, core)
        return remote(
            next_send.at[side, goal],
            next_recv.at[side, own],
            next_ssem.at[side, d],
            next_rsem.at[side, d],
            where,
        )

    for side in range(2):
        count, lines = (ny, nx) if side == 0 else (nx, ny)
        own_line = x if side == 0 else y
        for step in range(1, lines + 1):
            line = turned(own_line, step, lines)
            b = y * nx + line if side == 0 else line * nx + x
            value = total[b, side * part : (side + 1) * part, :]
            for d in range(1, count):
                sender, move = first_wait(side, d, line)
                move.wait_recv()
                value = value + first_recv[side, sender, line].astype(F32)
            if step < lines:
                next_send[side, line] = value.astype(BF16)
                next_copy(side, step).start()
            else:
                next_total[side] = value

    for move in y_gain:
        move.wait_recv()
    gain_x[x] = gain_sum(gain_y, ny)
    x_gain = gain_exchange(gain_x, x, nx, lambda xx: device(y, xx, z, core), 2)
    for move in x_gain:
        move.start()

    def z_copy(goal):
        return remote(
            z_send.at[goal],
            z_recv.at[z],
            z_ssem.at[goal],
            z_rsem.at[z],
            device(y, x, core * z_half + goal, core),
        )

    for side in range(2):
        lines = nx if side == 0 else ny
        value = next_total[side]
        for d in range(1, lines):
            sender = turned(x if side == 0 else y, lines - d, lines)
            next_copy(side, d).wait_recv()
            value = value + next_recv[side, sender].astype(F32)
        for i in range(z_half // 2):
            goal = side * (z_half // 2) + i
            piece = value[i * z_rows : (i + 1) * z_rows]
            z_total[goal] = piece
            z_send[goal] = piece.astype(BF16)

            @pl.when(core * z_half + goal != z)
            def _():
                z_copy(goal).start()

    for move in x_gain:
        move.wait_recv()
    gain_z[z] = gain_sum(gain_x, nx)
    z_gain = gain_exchange(gain_z, z, nz, lambda zz: device(y, x, zz, core), 3)
    for move in z_gain:
        move.start()

    final = remote(
        final_send, final_recv, final_ssem, final_rsem, device(y, x, z, 1 - core)
    )
    owner = lax.div(z, z_half) == core
    final_rows = z_rows // CORES

    @pl.when(owner)
    def _():
        value = z_total[lax.rem(z, z_half)]
        for d in range(1, nz):
            sender = turned(z, d, nz)
            move = remote(
                z_send.at[0],
                z_recv.at[sender],
                z_ssem.at[0],
                z_rsem.at[sender],
                device(y, x, z, 1 - core),
            )
            move.wait_recv()
            value = value + z_recv[sender].astype(F32)
        value = value * inv_root
        lower = value[:final_rows]
        upper = value[final_rows:]
        mine = jnp.where(core == 0, lower, upper)
        final_send[...] = jnp.where(core == 0, upper, lower)
        final.start()
        out_ref[...] = mine
        final.wait_send()

    @pl.when(jnp.logical_not(owner))
    def _():
        final.wait_recv()
        out_ref[...] = final_recv[...]

    for move in z_gain:
        move.wait_recv()
    gout_ref[...] = gain_sum(gain_z, nz) * inv_root

    for move in core_gain + y_gain + x_gain + z_gain:
        move.wait_send()

    @pl.loop(0, blocks)
    def _(b):
        yy, xx = lax.div(b, nx), lax.rem(b, nx)
        core_copy(b).wait_send()

        @pl.when(yy != y)
        def _():
            first_copy(0, yy, xx).wait_send()

        @pl.when(xx != x)
        def _():
            first_copy(1, yy, xx).wait_send()

    for side in range(2):
        for d in range(1, nx if side == 0 else ny):
            next_copy(side, d).wait_send()
    for goal in range(z_half):

        @pl.when(core * z_half + goal != z)
        def _():
            z_copy(goal).wait_send()


def reduce_weights(mesh_sizes, normed, mixed, dqkv, cot, gain_part, inv_root):
    tm_size, inner = mesh_sizes
    tokens, width = normed.shape
    ny, nx = tm_size // X_HI, X_HI * X_LO
    nz = inner // (X_LO * CORES)
    left_width = 3 * width // tm_size
    block = 4 * width // tm_size
    rows = width // (X_LO * CORES)
    right = jnp.concatenate(
        [dqkv.reshape(tokens, tm_size, -1), cot.reshape(tokens, tm_size, -1)], axis=-1
    ).transpose(1, 0, 2)

    def cut(array):
        return array.T.reshape(X_LO, CORES, rows, tokens)

    part = rows // 2
    z_half = nz // CORES
    z_rows = rows // z_half
    final_rows = z_rows // CORES
    blocks = ny * nx
    most = max(nx, ny)
    vmem = pl.BlockSpec(memory_space=pltpu.VMEM)
    sizes = (ny, nx, nz, left_width, inv_root)
    dma = pltpu.SemaphoreType.DMA
    return pl.pallas_call(
        functools.partial(reduce_kernel, sizes),
        out_shape=(
            jax.ShapeDtypeStruct((final_rows, block), F32),
            jax.ShapeDtypeStruct((8, WIDE), F32),
        ),
        in_specs=[vmem] * 4,
        out_specs=(vmem,) * 2,
        scratch_shapes=[
            pltpu.VMEM((blocks, rows, block), BF16),
            pltpu.VMEM((blocks, rows, block), BF16),
            pltpu.VMEM((blocks, rows, block), F32),
            pltpu.VMEM((2, most, most, part, block), BF16),
            pltpu.VMEM((2, most, most, part, block), BF16),
            pltpu.VMEM((2, part, block), F32),
            pltpu.VMEM((2, most, part, block), BF16),
            pltpu.VMEM((2, most, part, block), BF16),
            pltpu.VMEM((z_half, z_rows, block), F32),
            pltpu.VMEM((z_half, z_rows, block), BF16),
            pltpu.VMEM((nz, z_rows, block), BF16),
            pltpu.VMEM((final_rows, block), F32),
            pltpu.VMEM((final_rows, block), F32),
            pltpu.VMEM((CORES, 8, WIDE), F32),
            pltpu.VMEM((ny, 8, WIDE), F32),
            pltpu.VMEM((nx, 8, WIDE), F32),
            pltpu.VMEM((nz, 8, WIDE), F32),
            dma((blocks,)),
            dma((blocks,)),
            dma((2, most, most)),
            dma((2, most, most)),
            dma((2, most)),
            dma((2, most)),
            dma((z_half,)),
            dma((nz,)),
            dma,
            dma,
            dma((4, nz)),
            dma((4, nz)),
        ],
        compiler_params=pltpu.CompilerParams(
            collective_id=1, has_side_effects=True, vmem_limit_bytes=48 * 2**20
        ),
        name="weight_reduction",
    )(cut(normed), cut(mixed), right, gain_part)


def shards(frames, norm_gain, w_qkv, w_out, cotangent):
    mesh_sizes = (lax.axis_size("tm"), lax.axis_size("inner"))
    tm_size, inner = mesh_sizes
    width = frames.shape[-1]
    tokens = frames.shape[0] * frames.shape[1]
    tokens_all = tokens * tm_size * inner
    x = frames.reshape(tokens, width)
    cot = cotangent.reshape(tokens, width)
    block_out, frames_grad, normed, mixed, dqkv, gain_part = attention(
        mesh_sizes, x, norm_gain.reshape(1, width), w_qkv, w_out, cot
    )
    inv_root = 1.0 / math.sqrt(tokens_all)
    weights, gain_sum = reduce_weights(
        mesh_sizes, normed, mixed, dqkv, cot, gain_part, inv_root
    )
    cut = 3 * width // tm_size
    share = width // inner
    gain_share = lax.dynamic_slice_in_dim(
        gain_sum.reshape(-1), lax.axis_index("inner") * share, share
    )
    return (
        block_out.reshape(frames.shape),
        frames_grad.reshape(frames.shape),
        weights[:, :cut],
        weights[:, cut:],
        gain_share,
    )


def solution(mesh):
    in_specs = (P(("tm", "inner"), None, None), P(), P(), P(), P(("tm", "inner"), None, None))
    out_specs = (
        P(("tm", "inner"), None, None),
        P(("tm", "inner"), None, None),
        P("inner", "tm"),
        P("inner", "tm"),
        P("inner"),
    )
    return jax.shard_map(shards, mesh=mesh, in_specs=in_specs, out_specs=out_specs, check_vma=False)
```

time: 822 us -> 160 us (0.19); the launches traced: 813 us -> 159 us
  local copies, waits for them, and re-layouts: 280 us -> 10.7 us
  waiting for transfers between devices: 226 us -> 0 us
  Pallas kernels: 0 us -> 146 us
  other arithmetic: 121 us -> 1.38 us
  blocking collectives: 116 us -> 0 us
  starting transfers between devices: 37.9 us -> 0 us
  matrix products: 16.8 us -> 0 us
  between operations: 15.1 us -> 0.73 us
    unnamed x6 -> x0, waiting for transfers between devices: 155 us -> none
    pallas_call x0 -> x2, Pallas kernels: none -> 146 us  [the longest x1 106 us: attention(): pl.pallas_call(functools.partial(attention_kernel, sizes), out_shape=(jax...]
    mul x36 -> x0, local copies, waits for them, and re-layouts: 93.2 us -> none  [the longest x18 50.4 us: attend_back(): query_grad = query_grad + score_w * key_h]
    reshape x22 -> x2, local copies, waits for them, and re-layouts: 54.6 us -> 2.11 us  [the longest x1 1.27 us: shards(): norm_gain.reshape(1, width)]
    unnamed x93 -> x12, local copies, waits for them, and re-layouts: 52.3 us -> 2.43 us
    unnamed x1 -> x0, blocking collectives: 49.7 us -> none
    scatter-add x17 -> x0, other arithmetic: 48.2 us -> none  [the longest x8 24.7 us: attend_back(): key_grad = key_grad.at[offset:offset + held_frames].add(score_w * query_h)]
    reduce_scatter x2 -> x0, waiting for transfers between devices: 47.4 us -> none  [the longest x1 47.4 us: shards(): lax.psum_scatter(qkv_grad, 'inner', scatter_dimension=0, tiled=True)]
  transfers between devices with their start and end apart: 11 -> 0, of which waited for: 5 -> 0; matrix products, arithmetic and copies ran while one was open for 19% -> 0% of each run, Pallas kernels for 0% -> 0%
where the time goes in v1:
time: 160 us; the launch traced here: 159 us
  Pallas kernels  146 us (91%)
  local copies, waits for them, and re-layouts  10.7 us (7%)
    pallas_call x1, Pallas kernels, attention(): pl.pallas_call(functools.partial(attention_kernel, sizes), out_shape=(jax...  106 us
    pallas_call x1, Pallas kernels, reduce_weights(): pl.pallas_call(functools.partial(reduce_kernel, sizes), out_shape=(jax.Sh...  40.2 us

profile of v1, /device:TPU:32, one launch (start us, length us, event | category | flops | bytes accessed | tf_op | source)
XLA Modules:
  0.0 159.0 jit_solution(12963425275657756929)
XLA Ops:
  0.6 1.3 reshape.38.gain_ref
  1.9 106.0 %windowed_attention.1 = (bf16[256,768]{1,0:T(8,128)(2,1)}, bf16[256,768]{1,0:T(8,128)(2,1)}, bf16[256,768]{1,0:T(8,128)(2,1)}, bf16[256,768]{1,0:T(8,128)(2,1)},...) custom-call(bf16[256,768]{1,0:T(8,128)(2,1)} %bitcast.21, f32[1,768]{1,0:T(1,128)} %reshape.38.gain_ref, ...), custom_call_target="tpu_custom_call" | custom-call | tf_op jit(solution)/shard_map/windowed_attention/pallas_call | solution.py:280
  107.9 1.6 copy.14
  109.5 0.0 copy-start.1
  109.5 0.8 copy.16
  110.3 0.1 copy-done.1
  110.5 0.2 copy.15
  110.7 1.0 copy.17
  111.6 1.4 maximum_bitcast_fusion.right_ref
  113.0 0.0 copy-start
  113.0 1.2 copy.12
  114.2 0.0 copy-start.3
  114.2 1.2 copy.13
  115.4 0.0 copy-done
  115.5 0.0 copy-start.2
  115.5 40.2 %weight_reduction.1 = (f32[24,384]{1,0:T(8,128)S(1)}, f32[8,128]{1,0:T(8,128)S(1)}) custom-call(bf16[2,2,192,256]{3,2,1,0:T(8,128)(2,1)S(1)} %bitcast.14, bf16[2,2,192,256]{3,2,1,0:T(8,128)(2,1)S(1)} %bitcast.15, bf16[8,256,384]{2,1,0:T(8,128)(2,1)S(1)} %maximum_bitcast_fusion.right_ref, f32[8,128]{1,0:T(8,128)S(1)} %copy-done), custom_call_target="tpu_custom_call" | custom-call | tf_op jit(solution)/shard_map/weight_reduction/pallas_call | solution.py:656
  155.7 0.6 dynamic_slice.3
  156.2 0.7 slice.7
  156.9 0.0 copy-done.3
  156.9 0.7 copy.21
  157.7 0.0 copy-done.2
  157.7 0.7 copy.22
  158.4 0.6 copy.23
Async XLA Ops:
  109.5 1.0 copy-start.1
  113.0 2.4 %copy-start = (f32[8,128]{1,0:T(8,128)S(1)}, f32[8,128]{1,0:T(8,128)}, u32[]{:S(2)}) copy-start(f32[8,128]{1,0:T(8,128)} %get-tuple-element.18.gain_ref) | copy-start | bytes 12292
  114.2 42.7 %copy-start.3 = (bf16[256,768]{1,0:T(8,128)(2,1)S(1)}, bf16[256,768]{1,0:T(8,128)(2,1)}, u32[]{:S(2)}) copy-start(bf16[256,768]{1,0:T(8,128)(2,1)} %get-tuple-element.13) | copy-start | bytes 1179652
  115.5 42.2 %copy-start.2 = (bf16[256,768]{1,0:T(8,128)(2,1)S(1)}, bf16[256,768]{1,0:T(8,128)(2,1)}, u32[]{:S(2)}) copy-start(bf16[256,768]{1,0:T(8,128)(2,1)} %get-tuple-element.14) | copy-start | bytes 1179652

commit v2 on v0

v2 whole, which is shorter than its diff:
```python
import functools
import math

import jax
import jax.numpy as jnp
from jax import lax
from jax.experimental import pallas as pl
from jax.experimental.pallas import tpu as pltpu
from jax.sharding import PartitionSpec as P

HEAD_DIM = 64
WINDOW = 4
CLIP_MAX = 256
EPSILON = 1e-06
SPAN = 2 * WINDOW + 1
WIDE = 128
ROWS = 64
CORES = 2
X_LO = 2
X_HI = 2
MESH = pl.DeviceIdType.MESH
F32 = jnp.float32
BF16 = jnp.bfloat16


def dot(a, b, dims=((1,), (0,))):
    return lax.dot_general(a, b, (dims, ((), ())), preferred_element_type=F32)


def split(wide_vals):
    high = wide_vals.astype(BF16)
    low = (wide_vals - high.astype(F32)).astype(BF16)
    return jnp.concatenate([high, low], axis=1)


def remote(source, target, ssem, rsem, where):
    return pltpu.make_async_remote_copy(
        src_ref=source,
        dst_ref=target,
        send_sem=ssem,
        recv_sem=rsem,
        device_id=where,
        device_id_type=MESH,
    )


def turned(value, step, count):
    return lax.rem(value + step, count)


def block_kernel(
    sizes,
    x_ref,
    gain_ref,
    cot_ref,
    wqkv_hbm,
    wout_hbm,
    bo_ref,
    fg_ref,
    wq_ref,
    wo_ref,
    gout_ref,
    wqkv_ref,
    wout_ref,
    xn,
    halo,
    comp,
    rcomp,
    wd,
    stack,
    dqkv_ref,
    unit,
    spread,
    ones,
    pick,
    spill,
    right_own,
    right_other,
    nleft_own,
    nleft_other,
    mleft_own,
    mleft_other,
    left_t,
    total,
    f0_send,
    f0_recv,
    f1_send,
    f1_recv,
    n_total,
    n0_send,
    n0_recv,
    n1_send,
    n1_recv,
    z_total,
    z_send,
    z_recv,
    final_send,
    final_recv,
    gain_core,
    gain_y,
    gain_x,
    gain_z,
    load_sem,
    send_sem,
    recv_sem,
    csend_sem,
    crecv_sem,
    gsend_sem,
    grecv_sem,
    f0_ssem,
    f0_rsem,
    f1_ssem,
    f1_rsem,
    n0_ssem,
    n0_rsem,
    n1_ssem,
    n1_rsem,
    z_ssem,
    z_rsem,
    final_ssem,
    final_rsem,
    gain_ssem,
    gain_rsem,
):
    tm_size, inner, clip, inv_root = sizes
    frames_all = tm_size * inner
    tokens, width = x_ref.shape
    pairs = width // WIDE
    parts = tokens // ROWS
    ny, nx = tm_size // X_HI, X_HI * X_LO
    nz = inner // (X_LO * CORES)
    half_width = width // CORES
    share = 3 * width // tm_size
    block = 4 * width // tm_size
    side_rows = half_width // 2
    z_rows = half_width // nz
    final_rows = z_rows // CORES

    tm_at = lax.axis_index("tm")
    inner_at = lax.axis_index("inner")
    f = tm_at * inner + inner_at
    odd = lax.rem(f, 2)
    core = lax.rem(inner_at, CORES)
    z = lax.rem(lax.div(inner_at, CORES), nz)
    x_lo = lax.div(inner_at, CORES * nz)
    x_hi = lax.rem(tm_at, X_HI)
    x = x_hi * X_LO + x_lo
    y = lax.div(tm_at, X_HI)
    active = x_lo == core

    def at(offset):
        g = lax.rem(f + offset + frames_all, frames_all)
        return (lax.div(g, inner), lax.rem(g, inner))

    def device(yy, xx, zz, cc):
        return (
            yy * X_HI + lax.div(xx, X_LO),
            (lax.rem(xx, X_LO) * nz + zz) * CORES + cc,
        )

    partner = device(y, x, z, 1 - core)
    others = [j for j in range(-WINDOW, WINDOW + 1) if j != 0]
    peers = [at(j) for j in others]
    peers += [device(turned(y, d, ny), x, z, core) for d in range(1, ny)]
    peers += [device(y, turned(x, d, nx), z, core) for d in range(1, nx)]
    peers += [device(y, x, turned(z, d, nz), core) for d in range(1, nz)]
    barrier = pltpu.get_barrier_semaphore()
    for peer in peers:
        pl.semaphore_signal(barrier, inc=1, device_id=peer, device_id_type=MESH)

    load_qkv = pltpu.make_async_copy(wqkv_hbm, wqkv_ref, load_sem.at[0])
    load_out = pltpu.make_async_copy(wout_hbm, wout_ref, load_sem.at[1])
    load_qkv.start()
    load_out.start()

    wide_vals = x_ref[...].astype(F32)
    center = wide_vals - jnp.mean(wide_vals, axis=-1, keepdims=True)
    spread_one = lax.rsqrt(jnp.mean(center * center, axis=-1, keepdims=True) + EPSILON)
    unit_rows = center * spread_one
    unit[...] = unit_rows
    spread[...] = spread_one
    normed = (unit_rows * gain_ref[...]).astype(BF16)
    for p in range(parts):
        rows = slice(p * ROWS, (p + 1) * ROWS)
        xn[2, p, :, 0:width] = normed[rows]
        xn[2, p, :, width : 2 * width] = cot_ref[rows, :]
    for i in range(CORES):
        nleft_own[i] = normed[:, i * half_width : (i + 1) * half_width]

    def columns(c, part, size=WIDE):
        return pl.ds(pl.multiple_of(part * width + c * size, size), size)

    def copy(p, k):
        if k < 4:
            source = xn.at[(2, 2, 1, 3)[k], p]
            target = xn.at[(1, 3, 0, 4)[k], p]
            where = at((2, -2, 2, -2)[k])
        else:
            slot = (4, 2, 6, 8 - 8 * odd)[k - 4]
            source = halo.at[p, slot]
            target = halo.at[p, slot - 1 + 2 * odd]
            where = partner
        return remote(source, target, send_sem.at[p, k], recv_sem.at[p, k], where)

    def comp_copy(p, j):
        k = j + WINDOW
        return remote(
            comp.at[p, k],
            rcomp.at[p, SPAN - 1 - k],
            csend_sem.at[p, k],
            crecv_sem.at[p, k],
            at(j),
        )

    normed_copy = remote(
        nleft_own.at[1 - core], nleft_other, gsend_sem.at[0, 2], grecv_sem.at[0, 2], partner
    )

    def left_copy(p):
        return remote(
            mleft_own.at[1 - core, p],
            mleft_other.at[p],
            gsend_sem.at[p, 0],
            grecv_sem.at[p, 0],
            partner,
        )

    def right_copy(p):
        return remote(
            right_own.at[p], right_other.at[p], gsend_sem.at[p, 1], grecv_sem.at[p, 1], partner
        )

    pl.semaphore_wait(barrier, len(peers))

    @pl.loop(0, min(2, parts))
    def _(p):
        copy(p, 0).start()
        copy(p, 1).start()

    normed_copy.start()

    row_at = lax.broadcasted_iota(jnp.int32, (2 * WIDE, WIDE), 0)
    lane_at = lax.broadcasted_iota(jnp.int32, (2 * WIDE, WIDE), 1)
    same = (lax.rem(row_at, WIDE) // HEAD_DIM) == (lane_at // HEAD_DIM)
    ones[...] = jnp.where(same, 1.0, 0.0).astype(BF16)
    row_at = lax.broadcasted_iota(jnp.int32, pick.shape, 0)
    lane_at = lax.broadcasted_iota(jnp.int32, pick.shape, 1)
    pick[...] = jnp.where(row_at == lane_at * HEAD_DIM, 1.0, 0.0).astype(BF16)
    row_at = lax.broadcasted_iota(jnp.int32, spill.shape, 0)
    lane_at = lax.broadcasted_iota(jnp.int32, spill.shape, 1)
    spill[...] = jnp.where(lane_at // HEAD_DIM == row_at, 1.0, 0.0).astype(BF16)

    def place(p, value, start, stride, lead):
        left = value.shape[1]
        taken = 0
        while taken < left:
            t = (start + taken) // stride
            into = start + taken - t * stride
            count = min(left - taken, stride - into)
            right_own[p, t, :, lead + into : lead + into + count] = value[:, taken : taken + count]
            taken += count

    for p in range(parts):
        for m in range(pairs):
            value = cot_ref[p * ROWS : (p + 1) * ROWS, m * WIDE : (m + 1) * WIDE]
            place(p, value, m * WIDE, width // tm_size, share)

    load_qkv.wait()
    load_out.wait()

    def project(rows_in, put):
        for part in range(3):
            weight = wqkv_ref[:, part * width : (part + 1) * width]
            put(part, dot(rows_in[:, 0:width], weight).astype(BF16))
        put(3, dot(rows_in[:, width : 2 * width], wout_ref[...], ((1,), (1,))).astype(BF16))

    def put_own(part, value):
        for p in range(parts):
            halo[p, 4, :, part * width : (part + 1) * width] = value[p * ROWS : (p + 1) * ROWS]

    project(xn[2].reshape(tokens, 2 * width), put_own)

    @pl.loop(0, parts)
    def _(p):
        copy(p, 4).start()

    def relay(p):
        copy(p, 0).wait_recv()
        copy(p, 2).start()
        copy(p, 1).wait_recv()
        copy(p, 3).start()

    def project_others(p):
        copy(p, 2).wait_recv()
        copy(p, 3).wait_recv()
        rows_in = jnp.concatenate([xn[1, p], xn[3, p], xn[0, p], xn[4, p]], axis=0)

        def put(part, value):
            for i, k in enumerate((2, 6, 0, 8)):
                halo[p, k, :, part * width : (part + 1) * width] = value[
                    i * ROWS : (i + 1) * ROWS
                ]

        project(rows_in, put)
        for k in (5, 6, 7):
            copy(p, k).start()

    def attend(p):
        for k in (4, 5, 6, 7):
            copy(p, k).wait_recv()
        rows = pl.ds(pl.multiple_of(p * ROWS, ROWS), ROWS)

        @pl.loop(0, pairs)
        def _(c):
            def load(k, part):
                return halo[p, k, :, columns(c, part)].astype(F32)

            query = load(4, 0)
            grad = load(4, 3)
            products = [split(query * load(k, 1)) for k in range(SPAN)]
            scores = dot(jnp.concatenate(products, axis=0), ones[...]) * (HEAD_DIM**-0.5)
            products = [split(grad * load(k, 2)) for k in range(SPAN)]
            dots = dot(jnp.concatenate(products, axis=0), ones[...])
            score = []
            for k in range(SPAN):
                g = f + (k - WINDOW)
                inside = (g >= 0) & (g < frames_all)
                inside = inside & (lax.div(g + clip, clip) == lax.div(f + clip, clip))
                cap = jnp.where(inside, 3e38, -1e30).astype(F32)
                score.append(jnp.minimum(scores[k * ROWS : (k + 1) * ROWS], cap))
            top = functools.reduce(jnp.maximum, score)
            raised = [jnp.exp(s - top) for s in score]
            scale = 1.0 / functools.reduce(jnp.add, raised)
            soft = [e * scale for e in raised]
            mixed = jnp.zeros((ROWS, WIDE), F32)
            centre = jnp.zeros((ROWS, WIDE), F32)
            weight_at = pl.ds(pl.multiple_of(c * 2 * WIDE, WIDE), WIDE)
            slope_at = pl.ds(pl.multiple_of(c * 2 * WIDE + WIDE, WIDE), WIDE)
            for k in range(SPAN):
                weight = soft[k].astype(BF16)
                wd[k, :, weight_at] = weight
                mixed += weight.astype(F32) * load(k, 2)
                centre += soft[k] * dots[k * ROWS : (k + 1) * ROWS]
            side = lax.div(c, pairs // CORES)
            mleft_own[side, p, :, columns(lax.rem(c, pairs // CORES), 0)] = mixed.astype(BF16)
            query_grad = jnp.zeros((ROWS, WIDE), F32)
            for k in range(SPAN):
                gap = dots[k * ROWS : (k + 1) * ROWS] - centre
                slope = (soft[k] * gap * (HEAD_DIM**-0.5)).astype(BF16)
                wd[k, :, slope_at] = slope
                query_grad += slope.astype(F32) * load(k, 1)
            dqkv_ref[rows, columns(c, 0)] = query_grad.astype(BF16)

        small = dot(wd[...].reshape(SPAN * ROWS, 2 * width), pick[...])
        for k in range(SPAN):
            packed = small[k * ROWS : k * ROWS + 16]
            for r in range(1, ROWS // 16):
                at_row = k * ROWS + r * 16
                packed += pltpu.roll(small[at_row : at_row + 16], 32 * r, 1)
            if k == WINDOW:
                rcomp[p, k] = packed.astype(BF16)
            else:
                comp[p, k] = packed.astype(BF16)
                comp_copy(p, k - WINDOW).start()

    def collect(p):
        for j in others:
            comp_copy(p, j).wait_recv()
        rows = pl.ds(pl.multiple_of(p * ROWS, ROWS), ROWS)
        for k in range(SPAN):
            packed = rcomp[p, k].astype(F32)
            for r in range(ROWS // 16):
                value = packed if r == 0 else pltpu.roll(packed, WIDE - 32 * r, 1)
                stack[k * ROWS + r * 16 : k * ROWS + (r + 1) * 16, :] = value.astype(BF16)

        @pl.loop(0, pairs)
        def _(c):
            wide = dot(stack[...], spill[:, columns(c, 0, 2 * WIDE)])
            key_grad = jnp.zeros((ROWS, WIDE), F32)
            value_grad = jnp.zeros((ROWS, WIDE), F32)
            for k in range(SPAN):
                piece = wide[k * ROWS : (k + 1) * ROWS]
                value_grad += piece[:, :WIDE] * halo[p, k, :, columns(c, 3)].astype(F32)
                key_grad += piece[:, WIDE:] * halo[p, k, :, columns(c, 0)].astype(F32)
            dqkv_ref[rows, columns(c, 1)] = key_grad.astype(BF16)
            dqkv_ref[rows, columns(c, 2)] = value_grad.astype(BF16)

        for m in range(3 * pairs):
            value = dqkv_ref[rows, m * WIDE : (m + 1) * WIDE]
            place(p, value, m * WIDE, share, 0)
        left_copy(p).start()
        right_copy(p).start()

    relay(0)

    @pl.when(parts > 2)
    def _():
        copy(2, 0).start()
        copy(2, 1).start()

    if parts > 1:
        relay(1)
    project_others(0)

    @pl.loop(0, parts)
    def _(p):
        @pl.when(p + 3 < parts)
        def _():
            copy(p + 3, 0).start()
            copy(p + 3, 1).start()

        @pl.when(p + 2 < parts)
        def _():
            relay(p + 2)

        attend(p)

        @pl.when(p + 1 < parts)
        def _():
            project_others(p + 1)

        collect(p)

    def f0_copy(yy, xh):
        return remote(
            f0_send.at[yy, xh],
            f0_recv.at[y, xh],
            f0_ssem.at[yy, xh],
            f0_rsem.at[y, xh],
            device(yy, x, z, core),
        )

    def f1_copy(yy, xh):
        return remote(
            f1_send.at[xh, yy],
            f1_recv.at[x, yy],
            f1_ssem.at[xh, yy],
            f1_rsem.at[x, yy],
            device(y, xh * X_LO + core, z, core),
        )

    normed_copy.wait_recv()
    left_t[0, :, 0:tokens] = nleft_own[core].T
    left_t[0, :, tokens : 2 * tokens] = nleft_other[...].T
    for p in range(parts):
        left_copy(p).wait_recv()
    left_t[1, :, 0:tokens] = mleft_own[core].reshape(tokens, half_width).T
    left_t[1, :, tokens : 2 * tokens] = mleft_other[...].reshape(tokens, half_width).T
    for p in range(parts):
        right_copy(p).wait_recv()

    @pl.loop(0, tm_size)
    def _(i):
        t = turned(i + X_HI, y * X_HI, tm_size)
        yy, xh = lax.div(t, X_HI), lax.rem(t, X_HI)
        right = jnp.concatenate(
            [right_own[p, t] for p in range(parts)] + [right_other[p, t] for p in range(parts)],
            axis=0,
        )
        first = dot(left_t[0], right)
        last = (block - 1) // WIDE * WIDE
        second = dot(left_t[1], right[:, last:])
        lane = lax.broadcasted_iota(jnp.int32, second.shape, 1)
        tail = jnp.where(lane < share - last, first[:, last:], second)
        total[t, :, 0:last] = first[:, :last]
        total[t, :, last:block] = tail
        f0_send[yy, xh, :, 0:last] = first[:side_rows, :last].astype(BF16)
        f0_send[yy, xh, :, last:block] = tail[:side_rows].astype(BF16)
        f1_send[xh, yy, :, 0:last] = first[side_rows:, :last].astype(BF16)
        f1_send[xh, yy, :, last:block] = tail[side_rows:].astype(BF16)

        @pl.when(yy != y)
        def _():
            f0_copy(yy, xh).start()

        @pl.when(xh * X_LO + core != x)
        def _():
            f1_copy(yy, xh).start()

    normed_grad = dot(dqkv_ref[...], wqkv_ref[...], ((1,), (1,)))
    unit_rows = unit[...]
    gain_part = jnp.sum(normed_grad * unit_rows, axis=0, keepdims=True)
    gain_core[core] = jnp.zeros((8, WIDE), F32)
    for i in range(pairs):
        gain_core[core, i : i + 1, :] = gain_part[:, i * WIDE : (i + 1) * WIDE]

    def gain_exchange(buffer, own, count, spot, slot):
        return [
            remote(
                buffer.at[own],
                buffer.at[own],
                gain_ssem.at[slot, d],
                gain_rsem.at[slot, d],
                spot(turned(own, d, count)),
            )
            for d in range(1, count)
        ]

    def gain_sum(buffer, count):
        return functools.reduce(jnp.add, [buffer[i] for i in range(count)])

    core_gain = gain_exchange(gain_core, core, CORES, lambda cc: device(y, x, z, cc), 0)
    y_gain = gain_exchange(gain_y, y, ny, lambda yy: device(yy, x, z, core), 1)
    x_gain = gain_exchange(gain_x, x, nx, lambda xx: device(y, xx, z, core), 2)
    z_gain = gain_exchange(gain_z, z, nz, lambda zz: device(y, x, zz, core), 3)
    for move in core_gain:
        move.start()

    scaled = normed_grad * gain_ref[...]
    mean_one = jnp.mean(scaled, axis=-1, keepdims=True)
    second = jnp.mean(scaled * unit_rows, axis=-1, keepdims=True)
    back = spread[...] * (scaled - mean_one - unit_rows * second)
    fg_ref[...] = (cot_ref[...].astype(F32) + back).astype(BF16)
    mixed_out = x_ref[...].astype(F32)
    for i in range(CORES):
        mixed_half = mleft_own[i].reshape(tokens, half_width)
        mixed_out += dot(mixed_half, wout_ref[i * half_width : (i + 1) * half_width, :])
    bo_ref[...] = mixed_out.astype(BF16)

    for move in core_gain:
        move.wait_recv()
    gain_y[y] = gain_sum(gain_core, CORES)
    for move in y_gain:
        move.start()

    def n0_copy(xh):
        return remote(
            n0_send.at[xh],
            n0_recv.at[x],
            n0_ssem.at[xh],
            n0_rsem.at[x],
            device(y, xh * X_LO + core, z, core),
        )

    def n1_copy(yy):
        return remote(
            n1_send.at[yy],
            n1_recv.at[y],
            n1_ssem.at[yy],
            n1_rsem.at[y],
            device(yy, x, z, core),
        )

    def z_copy(zz):
        return remote(
            z_send.at[zz], z_recv.at[z], z_ssem.at[zz], z_rsem.at[z], device(y, x, zz, core)
        )

    def arrived(buffer, spot, sem):
        remote(buffer.at[spot], buffer.at[spot], sem.at[spot], sem.at[spot], partner).wait_recv()
        return buffer[spot].astype(F32)

    for step in range(1, X_HI + 1):
        xh = turned(x_hi, step, X_HI)
        value = total[y * X_HI + xh, 0:side_rows, :]
        for d in range(1, ny):
            value = value + arrived(f0_recv, (turned(y, d, ny), xh), f0_rsem)
        goal = xh * X_LO + core

        @pl.when(goal != x)
        def _():
            n0_send[xh] = value.astype(BF16)
            n0_copy(xh).start()

        @pl.when(goal == x)
        def _():
            n_total[0] = value

    @pl.when(active)
    def _():
        for step in range(1, ny + 1):
            yy = turned(y, step, ny)
            value = total[yy * X_HI + x_hi, side_rows : 2 * side_rows, :]
            for d in range(1, nx):
                value = value + arrived(f1_recv, (turned(x, d, nx), yy), f1_rsem)
            if step < ny:
                n1_send[yy] = value.astype(BF16)
                n1_copy(yy).start()
            else:
                n_total[1] = value

    for move in y_gain:
        move.wait_recv()
    gain_x[x] = gain_sum(gain_y, ny)
    for move in x_gain:
        move.start()

    @pl.when(active)
    def _():
        for side in range(2):
            value = n_total[side]
            for d in range(1, nx if side == 0 else ny):
                if side == 0:
                    value = value + arrived(n0_recv, turned(x, d, nx), n0_rsem)
                else:
                    value = value + arrived(n1_recv, turned(y, d, ny), n1_rsem)
            for i in range(nz // 2):
                zz = side * (nz // 2) + i
                piece = value[i * z_rows : (i + 1) * z_rows]
                z_total[zz] = piece
                z_send[zz] = piece.astype(BF16)

                @pl.when(zz != z)
                def _():
                    z_copy(zz).start()

    for move in x_gain:
        move.wait_recv()
    gain_z[z] = gain_sum(gain_x, nx)
    for move in z_gain:
        move.start()

    final = remote(final_send, final_recv, final_ssem, final_rsem, partner)

    def deliver(value):
        last = share // WIDE * WIDE
        wq_ref[:, 0:last] = value[:, :last]
        tail = value[:, last : last + WIDE]
        wq_ref[:, last:share] = tail[:, : share - last]
        if share == last:
            wo_ref[...] = tail
        else:
            count = block - share
            wo_ref[...] = pltpu.roll(tail, WIDE - (share - last), 1)[:, :count]

    @pl.when(active)
    def _():
        value = z_total[z]
        for d in range(1, nz):
            value = value + arrived(z_recv, turned(z, d, nz), z_rsem)
        value = value * inv_root
        lower = value[:final_rows]
        upper = value[final_rows:]
        final_send[...] = jnp.where(core == 0, upper, lower)
        final.start()
        deliver(jnp.where(core == 0, lower, upper))

    @pl.when(jnp.logical_not(active))
    def _():
        final.wait_recv()
        deliver(final_recv[...])

    for move in z_gain:
        move.wait_recv()
    gout_ref[...] = gain_sum(gain_z, nz) * inv_root

    normed_copy.wait_send()
    for move in core_gain + y_gain + x_gain + z_gain:
        move.wait_send()

    @pl.loop(0, parts)
    def _(p):
        for k in range(8):
            copy(p, k).wait_send()
        for j in others:
            comp_copy(p, j).wait_send()
        left_copy(p).wait_send()
        right_copy(p).wait_send()

    for xh in range(X_HI):
        for yy in range(ny):

            @pl.when(yy != y)
            def _():
                f0_copy(yy, xh).wait_send()

            @pl.when(xh * X_LO + core != x)
            def _():
                f1_copy(yy, xh).wait_send()

        @pl.when(xh * X_LO + core != x)
        def _():
            n0_copy(xh).wait_send()

    @pl.when(active)
    def _():
        for yy in range(ny):

            @pl.when(yy != y)
            def _():
                n1_copy(yy).wait_send()

        for zz in range(nz):

            @pl.when(zz != z)
            def _():
                z_copy(zz).wait_send()

        final.wait_send()


def shards(frames, norm_gain, w_qkv, w_out, cotangent):
    tm_size, inner = lax.axis_size("tm"), lax.axis_size("inner")
    width = frames.shape[-1]
    tokens = frames.shape[0] * frames.shape[1]
    frames_all = tm_size * inner
    x = frames.reshape(tokens, width)
    cot = cotangent.reshape(tokens, width)
    gain = norm_gain.reshape(1, width)
    ny, nx = tm_size // X_HI, X_HI * X_LO
    nz = inner // (X_LO * CORES)
    parts = tokens // ROWS
    half = width // CORES
    share = 3 * width // tm_size
    block = 4 * width // tm_size
    side = half // 2
    z_rows = half // nz
    final_rows = z_rows // CORES
    inv_root = 1.0 / math.sqrt(tokens * frames_all)
    sizes = (tm_size, inner, min(CLIP_MAX, frames_all), inv_root)
    vmem = pl.BlockSpec(memory_space=pltpu.VMEM)
    hbm = pl.BlockSpec(memory_space=pl.ANY)
    dma = pltpu.SemaphoreType.DMA
    block_out, frames_grad, qkv_share, out_share, gain_sum = pl.pallas_call(
        functools.partial(block_kernel, sizes),
        out_shape=(
            jax.ShapeDtypeStruct((tokens, width), BF16),
            jax.ShapeDtypeStruct((tokens, width), BF16),
            jax.ShapeDtypeStruct((final_rows, share), F32),
            jax.ShapeDtypeStruct((final_rows, block - share), F32),
            jax.ShapeDtypeStruct((8, WIDE), F32),
        ),
        in_specs=[vmem, vmem, vmem, hbm, hbm],
        out_specs=(vmem,) * 5,
        scratch_shapes=[
            pltpu.VMEM(w_qkv.shape, BF16),
            pltpu.VMEM(w_out.shape, BF16),
            pltpu.VMEM((5, parts, ROWS, 2 * width), BF16),
            pltpu.VMEM((parts, SPAN, ROWS, 4 * width), BF16),
            pltpu.VMEM((parts, SPAN, 16, WIDE), BF16),
            pltpu.VMEM((parts, SPAN, 16, WIDE), BF16),
            pltpu.VMEM((SPAN, ROWS, 2 * width), BF16),
            pltpu.VMEM((SPAN * ROWS, WIDE), BF16),
            pltpu.VMEM((tokens, 3 * width), BF16),
            pltpu.VMEM((tokens, width), F32),
            pltpu.VMEM((tokens, 1), F32),
            pltpu.VMEM((2 * WIDE, WIDE), BF16),
            pltpu.VMEM((2 * width, WIDE), BF16),
            pltpu.VMEM((WIDE, 2 * width), BF16),
            pltpu.VMEM((parts, tm_size, ROWS, block), BF16),
            pltpu.VMEM((parts, tm_size, ROWS, block), BF16),
            pltpu.VMEM((CORES, tokens, half), BF16),
            pltpu.VMEM((tokens, half), BF16),
            pltpu.VMEM((CORES, parts, ROWS, half), BF16),
            pltpu.VMEM((parts, ROWS, half), BF16),
            pltpu.VMEM((2, half, 2 * tokens), BF16),
            pltpu.VMEM((tm_size, half, block), F32),
            pltpu.VMEM((ny, X_HI, side, block), BF16),
            pltpu.VMEM((ny, X_HI, side, block), BF16),
            pltpu.VMEM((X_HI, ny, side, block), BF16),
            pltpu.VMEM((nx, ny, side, block), BF16),
            pltpu.VMEM((2, side, block), F32),
            pltpu.VMEM((X_HI, side, block), BF16),
            pltpu.VMEM((nx, side, block), BF16),
            pltpu.VMEM((ny, side, block), BF16),
            pltpu.VMEM((ny, side, block), BF16),
            pltpu.VMEM((nz, z_rows, block), F32),
            pltpu.VMEM((nz, z_rows, block), BF16),
            pltpu.VMEM((nz, z_rows, block), BF16),
            pltpu.VMEM((final_rows, block), F32),
            pltpu.VMEM((final_rows, block), F32),
            pltpu.VMEM((CORES, 8, WIDE), F32),
            pltpu.VMEM((ny, 8, WIDE), F32),
            pltpu.VMEM((nx, 8, WIDE), F32),
            pltpu.VMEM((nz, 8, WIDE), F32),
            dma((2,)),
            dma((parts, 8)),
            dma((parts, 8)),
            dma((parts, SPAN)),
            dma((parts, SPAN)),
            dma((parts, 3)),
            dma((parts, 3)),
            dma((ny, X_HI)),
            dma((ny, X_HI)),
            dma((X_HI, ny)),
            dma((nx, ny)),
            dma((X_HI,)),
            dma((nx,)),
            dma((ny,)),
            dma((ny,)),
            dma((nz,)),
            dma((nz,)),
            dma,
            dma,
            dma((4, nz)),
            dma((4, nz)),
        ],
        compiler_params=pltpu.CompilerParams(
            collective_id=0, has_side_effects=True, vmem_limit_bytes=60 * 2**20
        ),
        name="attention_block",
    )(x, gain, cot, w_qkv, w_out)
    cut = width // inner
    gain_share = lax.dynamic_slice_in_dim(
        gain_sum.reshape(-1), lax.axis_index("inner") * cut, cut
    )
    return (
        block_out.reshape(frames.shape),
        frames_grad.reshape(frames.shape),
        qkv_share,
        out_share,
        gain_share,
    )


def solution(mesh):
    in_specs = (P(("tm", "inner"), None, None), P(), P(), P(), P(("tm", "inner"), None, None))
    out_specs = (
        P(("tm", "inner"), None, None),
        P(("tm", "inner"), None, None),
        P("inner", "tm"),
        P("inner", "tm"),
        P("inner"),
    )
    return jax.shard_map(shards, mesh=mesh, in_specs=in_specs, out_specs=out_specs, check_vma=False)
```

time: 822 us -> 123 us (0.15); the launches traced: 813 us -> 122 us
  local copies, waits for them, and re-layouts: 280 us -> 8.76 us
  waiting for transfers between devices: 226 us -> 0 us
  other arithmetic: 121 us -> 0 us
  blocking collectives: 116 us -> 0 us
  Pallas kernels: 0 us -> 113 us
  starting transfers between devices: 37.9 us -> 0 us
  matrix products: 16.8 us -> 0 us
  between operations: 15.1 us -> 0.65 us
    unnamed x6 -> x0, waiting for transfers between devices: 155 us -> none
    pallas_call x0 -> x1, Pallas kernels: none -> 113 us  [shards(): pl.pallas_call(functools.partial(block_kernel, sizes), out_shape=(jax.Sha...]
    mul x36 -> x0, local copies, waits for them, and re-layouts: 93.2 us -> none  [the longest x18 50.4 us: attend_back(): query_grad = query_grad + score_w * key_h]
    reshape x22 -> x1, local copies, waits for them, and re-layouts: 54.6 us -> 1.27 us  [shards(): gain = norm_gain.reshape(1, width)]
    unnamed x1 -> x0, blocking collectives: 49.7 us -> none
    scatter-add x17 -> x0, other arithmetic: 48.2 us -> none  [the longest x8 24.7 us: attend_back(): key_grad = key_grad.at[offset:offset + held_frames].add(score_w * query_h)]
    reduce_scatter x2 -> x0, waiting for transfers between devices: 47.4 us -> none  [the longest x1 47.4 us: shards(): lax.psum_scatter(qkv_grad, 'inner', scatter_dimension=0, tiled=True)]
    unnamed x93 -> x4, local copies, waits for them, and re-layouts: 52.3 us -> 6.22 us
  transfers between devices with their start and end apart: 11 -> 0, of which waited for: 5 -> 0; matrix products, arithmetic and copies ran while one was open for 19% -> 0% of each run, Pallas kernels for 0% -> 0%
where the time goes in v2:
time: 123 us; the launch traced here: 122 us
  Pallas kernels  113 us (92%)
  local copies, waits for them, and re-layouts  8.76 us (7%)
    pallas_call x1, Pallas kernels, shards(): pl.pallas_call(functools.partial(block_kernel, sizes), out_shape=(jax.Sha...  113 us
    unnamed x4, local copies, waits for them, and re-layouts  6.22 us

profile of v2, /device:TPU:32, one launch (start us, length us, event | category | flops | bytes accessed | tf_op | source)
XLA Modules:
  0.0 122.1 jit_solution(15925442907396549520)
XLA Ops:
  0.6 1.3 %reshape.29.gain_ref = f32[1,768]{1,0:T(1,128)} reshape(f32[768]{0:T(1024)} %param.6) | data formatting | bytes 6144 | tf_op jit(solution)/shard_map/reshape | solution.py:699
  1.9 112.7 %attention_block.1 = (bf16[256,768]{1,0:T(8,128)(2,1)}, bf16[256,768]{1,0:T(8,128)(2,1)}, f32[24,288]{1,0:T(8,128)}, f32[24,96]{1,0:T(8,128)}, f32[8,128]{1,0:T(8,128)}) custom-call(bf16[256,768]{1,0:T(8,128)(2,1)} %bitcast.5, f32[1,768]{1,0:T(1,128)} %reshape.29.gain_ref, bf16[256,768]{1,0:T(8,128)(2,1)} %bitcast.6, bf16[768,2304]{1,0:T(8,128)(2,1)} %wqkv_hbm.1, ...), custom_call_target="tpu_custom_call" | custom-call | tf_op jit(solution)/shard_map/attention_block/pallas_call | solution.py:714
  114.6 1.3 %dynamic_slice.3 = f32[24]{0:T(128)} dynamic-slice(f32[1024]{0:T(1024)} %bitcast.9, s32[]{:T(128)S(6)} %select_n.3), dynamic_slice_sizes={24} | dynamic-slice | bytes 196 | tf_op jit(solution)/shard_map/dynamic_slice | solution.py:794
  115.9 1.8 %copy.14 = bf16[1,256,768]{2,1,0:T(8,128)(2,1)} copy(bf16[1,256,768]{2,1,0:T(8,128)(2,1)} %bitcast.8) | data formatting | bytes 786432
  117.6 1.8 %copy.15 = bf16[1,256,768]{2,1,0:T(8,128)(2,1)} copy(bf16[1,256,768]{2,1,0:T(8,128)(2,1)} %bitcast.7) | data formatting | bytes 786432
  119.4 1.4 %copy.16 = f32[24,288]{1,0:T(8,128)} copy(f32[24,288]{1,0:T(8,128)} %get-tuple-element.22) | data formatting | bytes 55296
  120.8 1.3 %copy.17 = f32[24,96]{1,0:T(8,128)} copy(f32[24,96]{1,0:T(8,128)} %get-tuple-element.23) | data formatting | bytes 18432

commit v3 on v2

--- a/solution.py
+++ b/solution.py
@@ -100,6 +100,7 @@
     gain_y,
     gain_x,
     gain_z,
+    gain_last,
     load_sem,
     send_sem,
     recv_sem,
@@ -179,7 +180,8 @@
     unit_rows = center * spread_one
     unit[...] = unit_rows
     spread[...] = spread_one
-    normed = (unit_rows * gain_ref[...]).astype(BF16)
+    gain_row = gain_ref[...].reshape(1, width)
+    normed = (unit_rows * gain_row).astype(BF16)
     for p in range(parts):
         rows = slice(p * ROWS, (p + 1) * ROWS)
         xn[2, p, :, 0:width] = normed[rows]
@@ -316,11 +318,11 @@
                 return halo[p, k, :, columns(c, part)].astype(F32)
 
             query = load(4, 0)
-            grad = load(4, 3)
+            grad = halo[p, 4, :, columns(c, 3)]
             products = [split(query * load(k, 1)) for k in range(SPAN)]
             scores = dot(jnp.concatenate(products, axis=0), ones[...]) * (HEAD_DIM**-0.5)
-            products = [split(grad * load(k, 2)) for k in range(SPAN)]
-            dots = dot(jnp.concatenate(products, axis=0), ones[...])
+            products = [grad * halo[p, k, :, columns(c, 2)] for k in range(SPAN)]
+            dots = dot(jnp.concatenate(products, axis=0), ones[0:WIDE])
             score = []
             for k in range(SPAN):
                 g = f + (k - WINDOW)
@@ -391,35 +393,37 @@
         left_copy(p).start()
         right_copy(p).start()
 
+    def start_own(p):
+        copy(p, 0).start()
+        copy(p, 1).start()
+
     relay(0)
-
-    @pl.when(parts > 2)
-    def _():
-        copy(2, 0).start()
-        copy(2, 1).start()
-
-    if parts > 1:
-        relay(1)
+    start_own(2)
+    relay(1)
+    start_own(3)
     project_others(0)
 
     @pl.loop(0, parts)
     def _(p):
-        @pl.when(p + 3 < parts)
+        @pl.when(p == 0)
         def _():
-            copy(p + 3, 0).start()
-            copy(p + 3, 1).start()
-
-        @pl.when(p + 2 < parts)
+            relay(2)
+
+        attend(p)
+
+        @pl.when(p == 0)
         def _():
-            relay(p + 2)
-
-        attend(p)
+            relay(3)
 
         @pl.when(p + 1 < parts)
         def _():
             project_others(p + 1)
 
-        collect(p)
+        @pl.when(p > 0)
+        def _():
+            collect(p - 1)
+
+    collect(parts - 1)
 
     def f0_copy(yy, xh):
         return remote(
@@ -506,7 +510,7 @@
     for move in core_gain:
         move.start()
 
-    scaled = normed_grad * gain_ref[...]
+    scaled = normed_grad * gain_ref[...].reshape(1, width)
     mean_one = jnp.mean(scaled, axis=-1, keepdims=True)
     second = jnp.mean(scaled * unit_rows, axis=-1, keepdims=True)
     back = spread[...] * (scaled - mean_one - unit_rows * second)
@@ -642,7 +646,18 @@
 
     for move in z_gain:
         move.wait_recv()
-    gout_ref[...] = gain_sum(gain_z, nz) * inv_root
+    gain_last[...] = gain_sum(gain_z, nz) * inv_root
+    cut = width // inner
+    row_one = lax.div(inner_at * cut, WIDE)
+    lead = lax.rem(inner_at * cut, WIDE)
+    low = jnp.broadcast_to(gain_last[pl.ds(row_one, 1), :], (8, WIDE))
+    high = jnp.broadcast_to(gain_last[pl.ds(row_one + 1, 1), :], (8, WIDE))
+    lane = lax.broadcasted_iota(jnp.int32, (8, WIDE), 1)
+    shift = lax.rem(WIDE - lead, WIDE)
+    merged = jnp.where(
+        lane < WIDE - lead, pltpu.roll(low, shift, 1), pltpu.roll(high, shift, 1)
+    )
+    gout_ref[...] = merged[0:1, :cut]
 
     normed_copy.wait_send()
     for move in core_gain + y_gain + x_gain + z_gain:
@@ -689,6 +704,26 @@
         final.wait_send()
 
 
+def copy_kernel(*refs):
+    count = len(refs) // 2
+    for source, target in zip(refs[:count], refs[count:], strict=True):
+        target[...] = source[...].reshape(target.shape)
+
+
+def hand_over(*arrays):
+    vmem = pl.BlockSpec(memory_space=pltpu.VMEM)
+    shapes = [a.shape for a in arrays[:-1]] + [(arrays[-1].size,)]
+    return pl.pallas_call(
+        copy_kernel,
+        out_shape=tuple(
+            jax.ShapeDtypeStruct(shape, a.dtype) for shape, a in zip(shapes, arrays, strict=True)
+        ),
+        in_specs=[vmem] * len(arrays),
+        out_specs=(vmem,) * len(arrays),
+        name="hand_over",
+    )(*arrays)
+
+
 def shards(frames, norm_gain, w_qkv, w_out, cotangent):
     tm_size, inner = lax.axis_size("tm"), lax.axis_size("inner")
     width = frames.shape[-1]
@@ -696,7 +731,6 @@
     frames_all = tm_size * inner
     x = frames.reshape(tokens, width)
     cot = cotangent.reshape(tokens, width)
-    gain = norm_gain.reshape(1, width)
     ny, nx = tm_size // X_HI, X_HI * X_LO
     nz = inner // (X_LO * CORES)
     parts = tokens // ROWS
@@ -718,7 +752,7 @@
             jax.ShapeDtypeStruct((tokens, width), BF16),
             jax.ShapeDtypeStruct((final_rows, share), F32),
             jax.ShapeDtypeStruct((final_rows, block - share), F32),
-            jax.ShapeDtypeStruct((8, WIDE), F32),
+            jax.ShapeDtypeStruct((1, width // inner), F32),
         ),
         in_specs=[vmem, vmem, vmem, hbm, hbm],
         out_specs=(vmem,) * 5,
@@ -763,6 +797,7 @@
             pltpu.VMEM((ny, 8, WIDE), F32),
             pltpu.VMEM((nx, 8, WIDE), F32),
             pltpu.VMEM((nz, 8, WIDE), F32),
+            pltpu.VMEM((8, WIDE), F32),
             dma((2,)),
             dma((parts, 8)),
             dma((parts, 8)),
@@ -789,17 +824,14 @@
             collective_id=0, has_side_effects=True, vmem_limit_bytes=60 * 2**20
         ),
         name="attention_block",
-    )(x, gain, cot, w_qkv, w_out)
-    cut = width // inner
-    gain_share = lax.dynamic_slice_in_dim(
-        gain_sum.reshape(-1), lax.axis_index("inner") * cut, cut
-    )
+    )(x, norm_gain, cot, w_qkv, w_out)
+    outs = hand_over(block_out, frames_grad, qkv_share, out_share, gain_sum)
     return (
-        block_out.reshape(frames.shape),
-        frames_grad.reshape(frames.shape),
-        qkv_share,
-        out_share,
-        gain_share,
+        outs[0].reshape(frames.shape),
+        outs[1].reshape(frames.shape),
+        outs[2],
+        outs[3],
+        outs[4],
     )
 
 

time: 123 us -> 107 us (0.87)
  local copies, waits for them, and re-layouts: 8.76 us -> 0 us
  Pallas kernels: 113 us -> 105 us
    pallas_call x1, Pallas kernels: 113 us -> 103 us  [shards(): pl.pallas_call(functools.partial(block_kernel, sizes), out_shape=(jax.Sha...]
    unnamed x4 -> x0, local copies, waits for them, and re-layouts: 6.22 us -> none
    pallas_call x0 -> x1, Pallas kernels: none -> 2.05 us  [hand_over(): pl.pallas_call(copy_kernel, out_shape=tuple((jax.ShapeDtypeStruct(shape,...]
    dynamic_slice x1 -> x0, local copies, waits for them, and re-layouts: 1.27 us -> none  [shards(): lax.dynamic_slice_in_dim(gain_sum.reshape(-1), lax.axis_index('inner') *...]
    reshape x1 -> x0, local copies, waits for them, and re-layouts: 1.27 us -> none  [shards(): gain = norm_gain.reshape(1, width)]
where the time goes in v3:
time: 107 us; the launch traced here: 106 us
  Pallas kernels  105 us (98%)
    pallas_call x1, Pallas kernels, shards(): pl.pallas_call(functools.partial(block_kernel, sizes), out_shape=(jax.Sha...  103 us

profile of v3, /device:TPU:32, one launch (start us, length us, event | category | flops | bytes accessed | tf_op | source)
XLA Modules:
  0.0 105.5 jit_solution(13896773621697753285)
XLA Ops:
  0.6 102.9 %attention_block.1 = (bf16[256,768]{1,0:T(8,128)(2,1)}, bf16[256,768]{1,0:T(8,128)(2,1)}, f32[24,288]{1,0:T(8,128)}, f32[24,96]{1,0:T(8,128)}, f32[1,24]{1,0:T(1,128)}) custom-call(bf16[256,768]{1,0:T(8,128)(2,1)} %bitcast.4, f32[768]{0:T(1024)} %gain_ref.1, bf16[256,768]{1,0:T(8,128)(2,1)} %bitcast.5, bf16[768,2304]{1,0:T(8,128)(2,1)} %wqkv_hbm.1, ...), custom_call_target="tpu_custom_call" | custom-call | tf_op jit(solution)/shard_map/attention_block/pallas_call | solution.py:748
  103.5 2.0 %hand_over.1 = (bf16[256,768]{1,0:T(8,128)(2,1)}, bf16[256,768]{1,0:T(8,128)(2,1)}, f32[24,288]{1,0:T(8,128)}, f32[24,96]{1,0:T(8,128)}, f32[24]{0:T(128)}) custom-call(bf16[256,768]{1,0:T(8,128)(2,1)} %get-tuple-element.15.refs_0_, bf16[256,768]{1,0:T(8,128)(2,1)} %get-tuple-element.16.refs_1_, f32[24,288]{1,0:T(8,128)} %get-tuple-element.17.refs_2_, ...), custom_call_target="tpu_custom_call" | custom-call | tf_op jit(solution)/shard_map/hand_over/pallas_call | solution.py:716

commit v4 on v3

--- a/solution.py
+++ b/solution.py
@@ -15,6 +15,7 @@
 SPAN = 2 * WINDOW + 1
 WIDE = 128
 ROWS = 64
+COPIES = 17
 CORES = 2
 X_LO = 2
 X_HI = 2
@@ -174,20 +175,22 @@
     load_qkv.start()
     load_out.start()
 
-    wide_vals = x_ref[...].astype(F32)
-    center = wide_vals - jnp.mean(wide_vals, axis=-1, keepdims=True)
-    spread_one = lax.rsqrt(jnp.mean(center * center, axis=-1, keepdims=True) + EPSILON)
-    unit_rows = center * spread_one
-    unit[...] = unit_rows
-    spread[...] = spread_one
-    gain_row = gain_ref[...].reshape(1, width)
-    normed = (unit_rows * gain_row).astype(BF16)
-    for p in range(parts):
+    def normalize(p):
         rows = slice(p * ROWS, (p + 1) * ROWS)
-        xn[2, p, :, 0:width] = normed[rows]
+        wide_vals = x_ref[rows, :].astype(F32)
+        center = wide_vals - jnp.mean(wide_vals, axis=-1, keepdims=True)
+        variance = jnp.mean(center * center, axis=-1, keepdims=True)
+        spread_one = lax.rsqrt(variance + EPSILON)
+        unit_rows = center * spread_one
+        unit[rows, :] = unit_rows
+        spread[rows, :] = spread_one
+        normed = (unit_rows * gain_ref[...].reshape(1, width)).astype(BF16)
+        xn[2, p, :, 0:width] = normed
         xn[2, p, :, width : 2 * width] = cot_ref[rows, :]
-    for i in range(CORES):
-        nleft_own[i] = normed[:, i * half_width : (i + 1) * half_width]
+        for i in range(CORES):
+            nleft_own[i, rows, :] = normed[:, i * half_width : (i + 1) * half_width]
+
+    normalize(0)
 
     def columns(c, part, size=WIDE):
         return pl.ds(pl.multiple_of(part * width + c * size, size), size)
@@ -197,10 +200,16 @@
             source = xn.at[(2, 2, 1, 3)[k], p]
             target = xn.at[(1, 3, 0, 4)[k], p]
             where = at((2, -2, 2, -2)[k])
+        elif k == 4:
+            source = halo.at[p, 4]
+            target = halo.at[p, 3 + 2 * odd]
+            where = partner
         else:
-            slot = (4, 2, 6, 8 - 8 * odd)[k - 4]
-            source = halo.at[p, slot]
-            target = halo.at[p, slot - 1 + 2 * odd]
+            slot = (2, 6, 8 - 8 * odd)[(k - 5) % 3]
+            part = (k - 5) // 3
+            lanes = pl.ds(part * width, width)
+            source = halo.at[p, slot, :, lanes]
+            target = halo.at[p, slot - 1 + 2 * odd, :, lanes]
             where = partner
         return remote(source, target, send_sem.at[p, k], recv_sem.at[p, k], where)
 
@@ -234,17 +243,21 @@
 
     pl.semaphore_wait(barrier, len(peers))
 
-    @pl.loop(0, min(2, parts))
-    def _(p):
+    def start_own(p):
         copy(p, 0).start()
         copy(p, 1).start()
 
+    start_own(0)
+    normalize(1)
+    start_own(1)
+    for p in range(2, parts):
+        normalize(p)
     normed_copy.start()
 
     row_at = lax.broadcasted_iota(jnp.int32, (2 * WIDE, WIDE), 0)
     lane_at = lax.broadcasted_iota(jnp.int32, (2 * WIDE, WIDE), 1)
     same = (lax.rem(row_at, WIDE) // HEAD_DIM) == (lane_at // HEAD_DIM)
-    ones[...] = jnp.where(same, 1.0, 0.0).astype(BF16)
+    ones[...] = jnp.where(same, HEAD_DIM**-0.5, 0.0).astype(BF16)
     row_at = lax.broadcasted_iota(jnp.int32, pick.shape, 0)
     lane_at = lax.broadcasted_iota(jnp.int32, pick.shape, 1)
     pick[...] = jnp.where(row_at == lane_at * HEAD_DIM, 1.0, 0.0).astype(BF16)
@@ -262,11 +275,6 @@
             right_own[p, t, :, lead + into : lead + into + count] = value[:, taken : taken + count]
             taken += count
 
-    for p in range(parts):
-        for m in range(pairs):
-            value = cot_ref[p * ROWS : (p + 1) * ROWS, m * WIDE : (m + 1) * WIDE]
-            place(p, value, m * WIDE, width // tm_size, share)
-
     load_qkv.wait()
     load_out.wait()
 
@@ -282,9 +290,7 @@
 
     project(xn[2].reshape(tokens, 2 * width), put_own)
 
-    @pl.loop(0, parts)
-    def _(p):
-        copy(p, 4).start()
+    copy(0, 4).start()
 
     def relay(p):
         copy(p, 0).wait_recv()
@@ -295,6 +301,11 @@
     def project_others(p):
         copy(p, 2).wait_recv()
         copy(p, 3).wait_recv()
+
+        @pl.when(p + 1 < parts)
+        def _():
+            copy(p + 1, 4).start()
+
         rows_in = jnp.concatenate([xn[1, p], xn[3, p], xn[0, p], xn[4, p]], axis=0)
 
         def put(part, value):
@@ -303,16 +314,17 @@
                     i * ROWS : (i + 1) * ROWS
                 ]
 
+            for i in range(3):
+                copy(p, 5 + 3 * part + i).start()
+
         project(rows_in, put)
-        for k in (5, 6, 7):
-            copy(p, k).start()
 
     def attend(p):
-        for k in (4, 5, 6, 7):
+        for k in range(4, COPIES):
             copy(p, k).wait_recv()
         rows = pl.ds(pl.multiple_of(p * ROWS, ROWS), ROWS)
 
-        @pl.loop(0, pairs)
+        @pl.loop(0, pairs, unroll=pairs)
         def _(c):
             def load(k, part):
                 return halo[p, k, :, columns(c, part)].astype(F32)
@@ -320,7 +332,7 @@
             query = load(4, 0)
             grad = halo[p, 4, :, columns(c, 3)]
             products = [split(query * load(k, 1)) for k in range(SPAN)]
-            scores = dot(jnp.concatenate(products, axis=0), ones[...]) * (HEAD_DIM**-0.5)
+            scores = dot(jnp.concatenate(products, axis=0), ones[...])
             products = [grad * halo[p, k, :, columns(c, 2)] for k in range(SPAN)]
             dots = dot(jnp.concatenate(products, axis=0), ones[0:WIDE])
             score = []
@@ -348,7 +360,7 @@
             query_grad = jnp.zeros((ROWS, WIDE), F32)
             for k in range(SPAN):
                 gap = dots[k * ROWS : (k + 1) * ROWS] - centre
-                slope = (soft[k] * gap * (HEAD_DIM**-0.5)).astype(BF16)
+                slope = (soft[k] * gap).astype(BF16)
                 wd[k, :, slope_at] = slope
                 query_grad += slope.astype(F32) * load(k, 1)
             dqkv_ref[rows, columns(c, 0)] = query_grad.astype(BF16)
@@ -375,7 +387,7 @@
                 value = packed if r == 0 else pltpu.roll(packed, WIDE - 32 * r, 1)
                 stack[k * ROWS + r * 16 : k * ROWS + (r + 1) * 16, :] = value.astype(BF16)
 
-        @pl.loop(0, pairs)
+        @pl.loop(0, pairs, unroll=pairs)
         def _(c):
             wide = dot(stack[...], spill[:, columns(c, 0, 2 * WIDE)])
             key_grad = jnp.zeros((ROWS, WIDE), F32)
@@ -393,27 +405,36 @@
         left_copy(p).start()
         right_copy(p).start()
 
-    def start_own(p):
-        copy(p, 0).start()
-        copy(p, 1).start()
-
     relay(0)
     start_own(2)
+    for p in range(parts):
+        for m in range(pairs):
+            value = cot_ref[p * ROWS : (p + 1) * ROWS, m * WIDE : (m + 1) * WIDE]
+            place(p, value, m * WIDE, width // tm_size, share)
+
+    normed_copy.wait_recv()
+    left_t[0, :, 0:tokens] = nleft_own[core].T
+    left_t[0, :, tokens : 2 * tokens] = nleft_other[...].T
+
     relay(1)
     start_own(3)
     project_others(0)
 
     @pl.loop(0, parts)
     def _(p):
+        @pl.when((p > 0) & (p + 2 < parts))
+        def _():
+            relay(p + 2)
+
+        @pl.when((p > 0) & (p + 3 < parts))
+        def _():
+            start_own(p + 3)
+
+        attend(p)
+
         @pl.when(p == 0)
         def _():
             relay(2)
-
-        attend(p)
-
-        @pl.when(p == 0)
-        def _():
-            relay(3)
 
         @pl.when(p + 1 < parts)
         def _():
@@ -443,9 +464,6 @@
             device(y, xh * X_LO + core, z, core),
         )
 
-    normed_copy.wait_recv()
-    left_t[0, :, 0:tokens] = nleft_own[core].T
-    left_t[0, :, tokens : 2 * tokens] = nleft_other[...].T
     for p in range(parts):
         left_copy(p).wait_recv()
     left_t[1, :, 0:tokens] = mleft_own[core].reshape(tokens, half_width).T
@@ -665,7 +683,7 @@
 
     @pl.loop(0, parts)
     def _(p):
-        for k in range(8):
+        for k in range(COPIES):
             copy(p, k).wait_send()
         for j in others:
             comp_copy(p, j).wait_send()
@@ -799,8 +817,8 @@
             pltpu.VMEM((nz, 8, WIDE), F32),
             pltpu.VMEM((8, WIDE), F32),
             dma((2,)),
-            dma((parts, 8)),
-            dma((parts, 8)),
+            dma((parts, COPIES)),
+            dma((parts, COPIES)),
             dma((parts, SPAN)),
             dma((parts, SPAN)),
             dma((parts, 3)),

time: 107 us -> 101 us (0.944)
  Pallas kernels: 105 us -> 99.1 us
    pallas_call x1, Pallas kernels: 103 us -> 97 us  [shards(): pl.pallas_call(functools.partial(block_kernel, sizes), out_shape=(jax.Sha...]
where the time goes in v4:
time: 101 us; the launch traced here: 99.7 us
  Pallas kernels  99.1 us (98%)
    pallas_call x1, Pallas kernels, shards(): pl.pallas_call(functools.partial(block_kernel, sizes), out_shape=(jax.Sha...  97 us
    pallas_call x1, Pallas kernels, hand_over(): pl.pallas_call(copy_kernel, out_shape=tuple((jax.ShapeDtypeStruct(shape,...  2.05 us

profile of v4, /device:TPU:32, one launch (start us, length us, event | category | flops | bytes accessed | tf_op | source)
XLA Modules:
  0.0 99.7 jit_solution(7712645179634112193)
XLA Ops:
  0.6 97.0 %attention_block.1 = (bf16[256,768]{1,0:T(8,128)(2,1)}, bf16[256,768]{1,0:T(8,128)(2,1)}, f32[24,288]{1,0:T(8,128)}, f32[24,96]{1,0:T(8,128)}, f32[1,24]{1,0:T(1,128)}) custom-call(bf16[256,768]{1,0:T(8,128)(2,1)} %bitcast.4, f32[768]{0:T(1024)} %gain_ref.1, bf16[256,768]{1,0:T(8,128)(2,1)} %bitcast.5, bf16[768,2304]{1,0:T(8,128)(2,1)} %wqkv_hbm.1, ...), custom_call_target="tpu_custom_call" | custom-call | tf_op jit(solution)/shard_map/attention_block/pallas_call | solution.py:766
  97.7 2.0 %hand_over.1 = (bf16[256,768]{1,0:T(8,128)(2,1)}, bf16[256,768]{1,0:T(8,128)(2,1)}, f32[24,288]{1,0:T(8,128)}, f32[24,96]{1,0:T(8,128)}, f32[24]{0:T(128)}) custom-call(bf16[256,768]{1,0:T(8,128)(2,1)} %get-tuple-element.15.refs_0_, bf16[256,768]{1,0:T(8,128)(2,1)} %get-tuple-element.16.refs_1_, f32[24,288]{1,0:T(8,128)} %get-tuple-element.17.refs_2_, ...), custom_call_target="tpu_custom_call" | custom-call | tf_op jit(solution)/shard_map/hand_over/pallas_call | solution.py:734

commit v5 on v4

--- a/solution.py
+++ b/solution.py
@@ -15,7 +15,7 @@
 SPAN = 2 * WINDOW + 1
 WIDE = 128
 ROWS = 64
-COPIES = 17
+COPIES = 21
 CORES = 2
 X_LO = 2
 X_HI = 2
@@ -196,17 +196,19 @@
         return pl.ds(pl.multiple_of(part * width + c * size, size), size)
 
     def copy(p, k):
-        if k < 4:
-            source = xn.at[(2, 2, 1, 3)[k], p]
-            target = xn.at[(1, 3, 0, 4)[k], p]
-            where = at((2, -2, 2, -2)[k])
-        elif k == 4:
+        if k < 8:
+            way = k // 2
+            rows = pl.ds(k % 2 * (ROWS // 2), ROWS // 2)
+            source = xn.at[(2, 2, 1, 3)[way], p, rows]
+            target = xn.at[(1, 3, 0, 4)[way], p, rows]
+            where = at((2, -2, 2, -2)[way])
+        elif k == 8:
             source = halo.at[p, 4]
             target = halo.at[p, 3 + 2 * odd]
             where = partner
         else:
-            slot = (2, 6, 8 - 8 * odd)[(k - 5) % 3]
-            part = (k - 5) // 3
+            slot = (2, 6, 8 - 8 * odd)[(k - 9) % 3]
+            part = (k - 9) // 3
             lanes = pl.ds(part * width, width)
             source = halo.at[p, slot, :, lanes]
             target = halo.at[p, slot - 1 + 2 * odd, :, lanes]
@@ -244,13 +246,20 @@
     pl.semaphore_wait(barrier, len(peers))
 
     def start_own(p):
-        copy(p, 0).start()
-        copy(p, 1).start()
+        for k in (0, 2, 1, 3):
+            copy(p, k).start()
+
+    def relay_half(p, half):
+        for way in range(2):
+            copy(p, 2 * way + half).wait_recv()
+            copy(p, 4 + 2 * way + half).start()
+
+    def relay(p):
+        relay_half(p, 0)
+        relay_half(p, 1)
 
     start_own(0)
-    normalize(1)
-    start_own(1)
-    for p in range(2, parts):
+    for p in range(1, parts):
         normalize(p)
     normed_copy.start()
 
@@ -275,6 +284,8 @@
             right_own[p, t, :, lead + into : lead + into + count] = value[:, taken : taken + count]
             taken += count
 
+    relay_half(0, 0)
+    start_own(1)
     load_qkv.wait()
     load_out.wait()
 
@@ -290,21 +301,15 @@
 
     project(xn[2].reshape(tokens, 2 * width), put_own)
 
-    copy(0, 4).start()
-
-    def relay(p):
-        copy(p, 0).wait_recv()
-        copy(p, 2).start()
-        copy(p, 1).wait_recv()
-        copy(p, 3).start()
+    copy(0, 8).start()
 
     def project_others(p):
-        copy(p, 2).wait_recv()
-        copy(p, 3).wait_recv()
+        for k in range(4, 8):
+            copy(p, k).wait_recv()
 
         @pl.when(p + 1 < parts)
         def _():
-            copy(p + 1, 4).start()
+            copy(p + 1, 8).start()
 
         rows_in = jnp.concatenate([xn[1, p], xn[3, p], xn[0, p], xn[4, p]], axis=0)
 
@@ -315,12 +320,12 @@
                 ]
 
             for i in range(3):
-                copy(p, 5 + 3 * part + i).start()
+                copy(p, 9 + 3 * part + i).start()
 
         project(rows_in, put)
 
     def attend(p):
-        for k in range(4, COPIES):
+        for k in range(8, COPIES):
             copy(p, k).wait_recv()
         rows = pl.ds(pl.multiple_of(p * ROWS, ROWS), ROWS)
 
@@ -405,7 +410,7 @@
         left_copy(p).start()
         right_copy(p).start()
 
-    relay(0)
+    relay_half(0, 1)
     start_own(2)
     for p in range(parts):
         for m in range(pairs):

time: 101 us -> 99.7 us (0.987)
    pallas_call x1, Pallas kernels: 97 us -> 96 us  [shards(): pl.pallas_call(functools.partial(block_kernel, sizes), out_shape=(jax.Sha...]
where the time goes in v5:
time: 99.7 us; the launch traced here: 98.7 us
  Pallas kernels  98.1 us (98%)
    pallas_call x1, Pallas kernels, shards(): pl.pallas_call(functools.partial(block_kernel, sizes), out_shape=(jax.Sha...  96 us
    pallas_call x1, Pallas kernels, hand_over(): pl.pallas_call(copy_kernel, out_shape=tuple((jax.ShapeDtypeStruct(shape,...  2.05 us

profile of v5, /device:TPU:32, one launch (start us, length us, event | category | flops | bytes accessed | tf_op | source)
XLA Modules:
  0.0 98.7 jit_solution(7202907033902501778)
XLA Ops:
  0.6 96.0 %attention_block.1 = (bf16[256,768]{1,0:T(8,128)(2,1)}, bf16[256,768]{1,0:T(8,128)(2,1)}, f32[24,288]{1,0:T(8,128)}, f32[24,96]{1,0:T(8,128)}, f32[1,24]{1,0:T(1,128)}) custom-call(bf16[256,768]{1,0:T(8,128)(2,1)} %bitcast.4, f32[768]{0:T(1024)} %gain_ref.1, bf16[256,768]{1,0:T(8,128)(2,1)} %bitcast.5, bf16[768,2304]{1,0:T(8,128)(2,1)} %wqkv_hbm.1, ...), custom_call_target="tpu_custom_call" | custom-call | tf_op jit(solution)/shard_map/attention_block/pallas_call | solution.py:771
  96.7 2.0 %hand_over.1 = (bf16[256,768]{1,0:T(8,128)(2,1)}, bf16[256,768]{1,0:T(8,128)(2,1)}, f32[24,288]{1,0:T(8,128)}, f32[24,96]{1,0:T(8,128)}, f32[24]{0:T(128)}) custom-call(bf16[256,768]{1,0:T(8,128)(2,1)} %get-tuple-element.15.refs_0_, bf16[256,768]{1,0:T(8,128)(2,1)} %get-tuple-element.16.refs_1_, f32[24,288]{1,0:T(8,128)} %get-tuple-element.17.refs_2_, ...), custom_call_target="tpu_custom_call" | custom-call | tf_op jit(solution)/shard_map/hand_over/pallas_call | solution.py:739

commit v6 on v5

--- a/solution.py
+++ b/solution.py
@@ -469,14 +469,14 @@
             device(y, xh * X_LO + core, z, core),
         )
 
+    left_t[1, :, 0:tokens] = mleft_own[core].reshape(tokens, half_width).T
     for p in range(parts):
         left_copy(p).wait_recv()
-    left_t[1, :, 0:tokens] = mleft_own[core].reshape(tokens, half_width).T
     left_t[1, :, tokens : 2 * tokens] = mleft_other[...].reshape(tokens, half_width).T
     for p in range(parts):
         right_copy(p).wait_recv()
 
-    @pl.loop(0, tm_size)
+    @pl.loop(0, tm_size, unroll=2)
     def _(i):
         t = turned(i + X_HI, y * X_HI, tm_size)
         yy, xh = lax.div(t, X_HI), lax.rem(t, X_HI)

time: 99.7 us -> 100 us (level)
  no operation moved by 1% of the time
where the time goes in v6:
time: 100 us; the launch traced here: 98.8 us
  Pallas kernels  98.2 us (98%)
    pallas_call x1, Pallas kernels, shards(): pl.pallas_call(functools.partial(block_kernel, sizes), out_shape=(jax.Sha...  96.1 us
    pallas_call x1, Pallas kernels, hand_over(): pl.pallas_call(copy_kernel, out_shape=tuple((jax.ShapeDtypeStruct(shape,...  2.05 us

profile of v6, /device:TPU:32, one launch (start us, length us, event | category | flops | bytes accessed | tf_op | source)
XLA Modules:
  0.0 98.8 jit_solution(2833972067199513401)
XLA Ops:
  0.6 96.1 %attention_block.1 = (bf16[256,768]{1,0:T(8,128)(2,1)}, bf16[256,768]{1,0:T(8,128)(2,1)}, f32[24,288]{1,0:T(8,128)}, f32[24,96]{1,0:T(8,128)}, f32[1,24]{1,0:T(1,128)}) custom-call(bf16[256,768]{1,0:T(8,128)(2,1)} %bitcast.4, f32[768]{0:T(1024)} %gain_ref.1, bf16[256,768]{1,0:T(8,128)(2,1)} %bitcast.5, bf16[768,2304]{1,0:T(8,128)(2,1)} %wqkv_hbm.1, ...), custom_call_target="tpu_custom_call" | custom-call | tf_op jit(solution)/shard_map/attention_block/pallas_call | solution.py:771
  96.8 2.0 %hand_over.1 = (bf16[256,768]{1,0:T(8,128)(2,1)}, bf16[256,768]{1,0:T(8,128)(2,1)}, f32[24,288]{1,0:T(8,128)}, f32[24,96]{1,0:T(8,128)}, f32[24]{0:T(128)}) custom-call(bf16[256,768]{1,0:T(8,128)(2,1)} %get-tuple-element.15.refs_0_, bf16[256,768]{1,0:T(8,128)(2,1)} %get-tuple-element.16.refs_1_, f32[24,288]{1,0:T(8,128)} %get-tuple-element.17.refs_2_, ...), custom_call_target="tpu_custom_call" | custom-call | tf_op jit(solution)/shard_map/hand_over/pallas_call | solution.py:739
